TPU v7x, 512 devices: a whole 4x4x16 slice. The times are simulated.
512 devices in a mesh: gx: 32 (over z, core), gy: 16 (over y, x).
Axes of the slice: x: 4, y: 4, z: 16, core: 2. Of those that a mesh axis runs over, the one named last changes fastest.
Arguments:
- nodes: bfloat16 [524288, 128], P(('gx', 'gy')), may hold values from -6 to 6
- edge_feat: bfloat16 [2097152, 128], P(('gx', 'gy')), may hold values from -6 to 6
- senders: int32 [2097152], P(('gx', 'gy')), may hold values from 0 to 1535
- receivers: int32 [2097152], P(('gx', 'gy')), may hold values from 0 to 1023
- send_lists: int32 [512, 4, 128], P(('gx', 'gy')), may hold values from 0 to 1023
- owner: int32 [524288], P(('gx', 'gy')), may hold values from 0 to 1023
- edge_live: int32 [512], P(('gx', 'gy')), may hold values from 1 to 4096, 1310720 in all
- cotangent: bfloat16 [524288, 128], P(('gx', 'gy')), may hold values from -6 to 6
- w_edge: bfloat16 [4, 128, 128], replicated, may hold values from -0.5 to 0.5
- w_node: bfloat16 [3, 128, 128], replicated, may hold values from -0.5 to 0.5
- w_coarse: bfloat16 [2, 128, 128], replicated, may hold values from -0.5 to 0.5
- biases: float32 [3, 128], replicated, may hold values from -3 to 3
Outputs:
- node_out: bfloat16 [524288, 128], P(('gx', 'gy'))
- d_nodes: bfloat16 [524288, 128], P(('gx', 'gy'))
- d_edges: bfloat16 [2097152, 128], P(('gx', 'gy'))
- weight_grads: float32 [9, 128, 128], replicated
- bias_grads: float32 [3, 128], replicated
Inputs may be any that keep to these rules, and one draw needn't show every extreme that they name: `senders`: a row of the partition's own 1024 cells or of its 512 halo rows. `receivers`: a cell of the partition. `send_lists`: cells of the sending partition. `owner`: a coarse cell of the cell's grid row. `edge_live`: some partition has all 4096 slots live.
All inputs are finite; a program needn't handle non-finite values. No bound on the sum of `edge_live` on one device may be relied on, other than what follows from the above.
Results may differ from a plain program's by a relative error of at most 0.014.
Values may be sent and summed in bfloat16 or wider, within the bound.
A program may use at most 64 MiB of HBM per device.

v0:
```python
import jax
import jax.numpy as jnp
from jax import lax
from jax.sharding import PartitionSpec as P


def padded(block, sides, width):
    for axis, dim in sides:
        count = lax.axis_size(axis)
        forward = [(i, i + 1) for i in range(count - 1)]
        backward = [(target, source) for source, target in forward]
        low = lax.ppermute(
            lax.slice_in_dim(block, block.shape[dim] - width, None, axis=dim), axis, forward
        )
        high = lax.ppermute(lax.slice_in_dim(block, 0, width, axis=dim), axis, backward)
        block = jnp.concatenate([low, block, high], axis=dim)
    return block


def matmul(left, right):
    return jnp.dot(left, right, preferred_element_type=jnp.float32)


def left_t(left, right):
    return lax.dot_general(
        left, right, (((0,), (0,)), ((), ())), preferred_element_type=jnp.float32
    )


def right_t(left, right):
    return lax.dot_general(
        left, right, (((1,), (1,)), ((), ())), preferred_element_type=jnp.float32
    )


def silu_slope(value):
    sigma = jax.nn.sigmoid(value)
    return sigma * (1.0 + value * (1.0 - sigma))


def edge_front(extended, edge_feat, senders, receivers, live, w_edge, biases):
    send_rows = extended[senders]
    recv_rows = extended[receivers]
    pre_edge = (
        matmul(send_rows, w_edge[0])
        + matmul(recv_rows, w_edge[1])
        + matmul(edge_feat, w_edge[2])
        + biases[0]
    )
    edge_hidden = jax.nn.silu(pre_edge).astype(jnp.bfloat16)
    message = matmul(edge_hidden, w_edge[3]) * live[:, None]
    return (send_rows, recv_rows, pre_edge, edge_hidden, message)


def node_front(nodes, message, receivers, w_node, biases):
    aggregated = jax.ops.segment_sum(message, receivers, num_segments=nodes.shape[0])
    agg_bf = aggregated.astype(jnp.bfloat16)
    pre_node = matmul(nodes, w_node[0]) + matmul(agg_bf, w_node[1]) + biases[1]
    node_hidden = jax.nn.silu(pre_node).astype(jnp.bfloat16)
    fine_state = nodes.astype(jnp.float32) + matmul(node_hidden, w_node[2])
    return (agg_bf, pre_node, node_hidden, fine_state)


def coarse_front(coarse_in, w_coarse, biases):
    coarse_bf = coarse_in.astype(jnp.bfloat16)
    pre_coarse = matmul(coarse_bf, w_coarse[0]) + biases[2]
    coarse_hidden = jax.nn.silu(pre_coarse).astype(jnp.bfloat16)
    coarse_out = matmul(coarse_hidden, w_coarse[1]).astype(jnp.bfloat16)
    return (coarse_bf, pre_coarse, coarse_hidden, coarse_out)


def coarse_back(pre_coarse, d_coarse_out, w_coarse):
    d_pre = right_t(d_coarse_out.astype(jnp.bfloat16), w_coarse[1]) * silu_slope(pre_coarse)
    d_coarse_in = right_t(d_pre.astype(jnp.bfloat16), w_coarse[0]).astype(jnp.bfloat16)
    return (d_pre, d_coarse_in)


def coarse_grads(coarse_bf, coarse_hidden, d_coarse_out, d_pre):
    first = left_t(coarse_bf, d_pre.astype(jnp.bfloat16))
    second = left_t(coarse_hidden, d_coarse_out.astype(jnp.bfloat16))
    return (jnp.stack([first, second]), jnp.sum(d_pre, axis=0))


def node_back(nodes, agg_bf, pre_node, node_hidden, d_fine, w_node):
    d_fine_bf = d_fine.astype(jnp.bfloat16)
    d_pre = right_t(d_fine_bf, w_node[2]) * silu_slope(pre_node)
    d_pre_bf = d_pre.astype(jnp.bfloat16)
    d_part = d_fine + right_t(d_pre_bf, w_node[0])
    d_agg = right_t(d_pre_bf, w_node[1])
    grads = jnp.stack(
        [left_t(nodes, d_pre_bf), left_t(agg_bf, d_pre_bf), left_t(node_hidden, d_fine_bf)]
    )
    return (d_part, d_agg, grads, jnp.sum(d_pre, axis=0))


def edge_back(
    send_rows,
    recv_rows,
    pre_edge,
    edge_hidden,
    edge_feat,
    senders,
    receivers,
    live,
    d_agg,
    w_edge,
    ext_count,
):
    d_message = (d_agg[receivers] * live[:, None]).astype(jnp.bfloat16)
    d_pre = right_t(d_message, w_edge[3]) * silu_slope(pre_edge)
    d_pre_bf = d_pre.astype(jnp.bfloat16)
    d_edges = right_t(d_pre_bf, w_edge[2]).astype(jnp.bfloat16)
    d_ext = jax.ops.segment_sum(right_t(d_pre_bf, w_edge[0]), senders, num_segments=ext_count)
    d_ext = d_ext + jax.ops.segment_sum(
        right_t(d_pre_bf, w_edge[1]), receivers, num_segments=ext_count
    )
    grads = jnp.stack(
        [
            left_t(send_rows, d_pre_bf),
            left_t(recv_rows, d_pre_bf),
            left_t(edge_feat, d_pre_bf),
            left_t(edge_hidden, d_message),
        ]
    )
    return (d_edges, d_ext, grads, jnp.sum(d_pre, axis=0))


def owner_sums(values, owner, start, count):
    inside = (owner >= start) & (owner < start + count)
    shifted = jnp.where(inside, owner, count)
    return jax.ops.segment_sum(values, shifted, num_segments=count + 1)[:count]


def pick_owned(owner, piece):
    columns = jnp.arange(piece.shape[0], dtype=jnp.int32)
    match = (owner[:, None] == columns[None, :]).astype(piece.dtype)
    return matmul(match, piece)


def body(
    nodes,
    edge_feat,
    senders,
    receivers,
    send_lists,
    owner,
    edge_live,
    cotangent,
    w_edge,
    w_node,
    w_coarse,
    biases,
):
    cells = nodes.shape[0]
    width = nodes.shape[1]
    halo_count = send_lists.shape[2]
    ext_count = cells + 4 * halo_count
    owned = cells // 16
    lists = send_lists[0]
    picked = nodes[lists]
    rows_ext = padded(jnp.stack([picked[0], picked[1]]), (("gx", 0),), 1)
    cols_ext = padded(jnp.stack([picked[2], picked[3]]), (("gy", 0),), 1)
    halo = jnp.concatenate([rows_ext[0], rows_ext[3], cols_ext[0], cols_ext[3]], axis=0)
    extended = jnp.concatenate([nodes, halo], axis=0)
    live = (jnp.arange(senders.shape[0], dtype=jnp.int32) < edge_live[0]).astype(jnp.float32)
    send_rows, recv_rows, pre_edge, edge_hidden, message = edge_front(
        extended, edge_feat, senders, receivers, live, w_edge, biases
    )
    agg_bf, pre_node, node_hidden, fine_state = node_front(
        nodes, message, receivers, w_node, biases
    )
    grad_out = cotangent.astype(jnp.float32)
    coarse_in = lax.psum_scatter(
        0.0625 * owner_sums(fine_state, owner, jnp.int32(0), owned * lax.axis_size("gy")),
        "gy",
        scatter_dimension=0,
        tiled=True,
    )
    coarse_bf, pre_coarse, coarse_hidden, coarse_out = coarse_front(coarse_in, w_coarse, biases)
    from_coarse = pick_owned(owner, lax.all_gather(coarse_out, "gy", axis=0, tiled=True))
    d_coarse_out = lax.psum_scatter(
        owner_sums(grad_out, owner, jnp.int32(0), owned * lax.axis_size("gy")),
        "gy",
        scatter_dimension=0,
        tiled=True,
    )
    d_pre_coarse, d_coarse_in = coarse_back(pre_coarse, d_coarse_out, w_coarse)
    coarse_w, coarse_b = coarse_grads(coarse_bf, coarse_hidden, d_coarse_out, d_pre_coarse)
    d_from_coarse = pick_owned(owner, lax.all_gather(d_coarse_in, "gy", axis=0, tiled=True))
    node_out = (fine_state + from_coarse).astype(jnp.bfloat16)
    d_fine = grad_out + 0.0625 * d_from_coarse
    d_part, d_agg, node_w, node_b = node_back(nodes, agg_bf, pre_node, node_hidden, d_fine, w_node)
    d_edges, d_ext, edge_w, edge_b = edge_back(
        send_rows,
        recv_rows,
        pre_edge,
        edge_hidden,
        edge_feat,
        senders,
        receivers,
        live,
        d_agg,
        w_edge,
        ext_count,
    )
    d_local = d_part + d_ext[:cells]
    d_halo = d_ext[cells:].reshape(4, halo_count, width)
    rows_back = padded(
        jnp.stack([d_halo[0], d_halo[1]]).astype(jnp.bfloat16), (("gx", 0),), 1
    ).astype(jnp.float32)
    cols_back = padded(
        jnp.stack([d_halo[2], d_halo[3]]).astype(jnp.bfloat16), (("gy", 0),), 1
    ).astype(jnp.float32)
    returned = jnp.concatenate([rows_back[0], rows_back[3], cols_back[0], cols_back[3]], axis=0)
    d_nodes = (
        d_local + jax.ops.segment_sum(returned, lists.reshape(-1), num_segments=cells)
    ).astype(jnp.bfloat16)
    weight_local = jnp.concatenate([edge_w, node_w, coarse_w], axis=0)
    bias_local = jnp.stack([edge_b, node_b, coarse_b])
    weight_grads, bias_grads = lax.psum((weight_local, bias_local), ("gx", "gy"))
    return (node_out, d_nodes, d_edges, weight_grads, bias_grads)


def solution(mesh):
    in_specs = (
        P(("gx", "gy"), None),
        P(("gx", "gy"), None),
        P(("gx", "gy")),
        P(("gx", "gy")),
        P(("gx", "gy"), None, None),
        P(("gx", "gy")),
        P(("gx", "gy")),
        P(("gx", "gy"), None),
        P(),
        P(),
        P(),
        P(),
    )
    out_specs = (P(("gx", "gy"), None), P(("gx", "gy"), None), P(("gx", "gy"), None), P(), P())
    return jax.shard_map(body, mesh=mesh, in_specs=in_specs, out_specs=out_specs, check_vma=False)
```

profile of v0, /device:TPU:1, one launch (start us, length us, event | category | flops | bytes accessed | tf_op | source)
XLA Modules:
  0.0 835.0 jit_solution(10601095402707271548)
XLA Ops:
  8.0 2.0 gather_fusion
  10.1 1.3 collective-permute-start.3
  11.4 4.6 collective-permute-start.2
  16.0 8.8 %collective-permute-start.1 = (bf16[1,128,128]{2,1,0:T(8,128)(2,1)S(1)}, bf16[1,128,128]{2,1,0:T(8,128)(2,1)S(1)}, u32[]{:S(2)}, u32[]{:S(2)}) collective-permute-start(bf16[1,128,128]{2,1,0:T(8,128)(2,1)S(1)} %get-tuple-element.21), channel_id=1, source_target_pairs={{16,0},{32,16},{48,32},{64,48},{80,64},{96,80},{112,96},{128,112},... | collective-permute-start | bytes 98312 | tf_op jit(solution)/shard_map/ppermute | solution.py:15
  24.8 1.9 collective-permute-start
  26.7 1.0 constant_dynamic-update-slice_fusion
  30.5 1.3 fusion.88
  31.8 1.0 fusion.66
  32.8 1.8 fusion.56
  35.3 12.1 %gather_fusion.2 = bf16[4096,128]{1,0:T(8,128)(2,1)S(1)} fusion(bf16[1536,128]{1,0:T(8,128)(2,1)S(1)} %bitcast_dynamic-update-slice_fusion, s32[4096]{0:T(1024)S(1)} %get-tuple-element.24), kind=kCustom, calls=%fused_computation.2 | custom fusion | bytes 2113536 | tf_op jit(solution)/shard_map/gather | solution.py:43
  47.4 15.0 %gather_fusion.1 = bf16[4096,128]{1,0:T(8,128)(2,1)} fusion(bf16[1536,128]{1,0:T(8,128)(2,1)S(1)} %bitcast_dynamic-update-slice_fusion, s32[4096]{0:T(1024)S(1)} %fusion.86), kind=kCustom, calls=%fused_computation.1 | custom fusion | bytes 2113536 | tf_op jit(solution)/shard_map/gather | solution.py:42
  64.4 1.8 fusion.1
  66.2 3.6 convolution_multiply_fusion.1
  69.8 22.8 %scatter_custom_fusion = f32[1024,128]{1,0:T(8,128)S(1)} fusion(s32[4096]{0:T(1024)} %param.15, f32[4096,128]{1,0:T(8,128)} %convolution_multiply_fusion.1, f32[]{:T(128)} %constant.6.clone.1), kind=kCustom, calls=%fused_computation.76 | custom fusion | flops 524288 | bytes 524800 | tf_op jit(solution)/shard_map/scatter-add | solution.py:56
  92.6 1.0 fusion.8
  93.5 0.8 copy-done.11
  94.4 1.8 convolution_add_fusion.2
  96.2 6.5 scatter_custom_fusion.1
  102.7 0.8 slice_multiply_fusion
  103.6 6.5 scatter_custom_fusion.2
  110.1 0.8 slice.163
  111.1 79.7 %reduce-scatter.3.cloned.1.call-done = f32[64,128]{1,0:T(8,128)} async-done(((f32[1024,128]{1,0:T(8,128)}), f32[64,128]{1,0:T(8,128)}) %reduce-scatter.3.cloned.1.call-update) | async-done | bytes 32784 | tf_op jit(solution)/shard_map/reduce_scatter | solution.py:173
  190.8 0.9 convolution_add_fusion.4
  192.3 1.5 convolution_convert_fusion.2
  193.8 88.7 %reduce-scatter.5.cloned.1.call-done = f32[64,128]{1,0:T(8,128)} async-done(((f32[1024,128]{1,0:T(8,128)}), f32[64,128]{1,0:T(8,128)}) %reduce-scatter.5.cloned.1.call-update) | async-done | bytes 32784 | tf_op jit(solution)/shard_map/reduce_scatter | solution.py:181
  282.5 1.0 fusion.100
  283.4 0.9 convolution_convert_fusion.1
  284.3 17.2 %all_gather.7 = bf16[1024,128]{1,0:T(8,128)(2,1)S(1)} all-gather(bf16[64,128]{1,0:T(8,128)(2,1)S(1)} %convolution_convert_fusion.1), channel_id=1, replica_groups=mesh['gx'=32,'gy'=16] {'gy'}, dimensions={0}, use_global_device_ids=true | all-gather | bytes 278528 | tf_op jit(solution)/shard_map/all_gather | solution.py:189
  301.5 1.8 fusion.10
  304.6 15.4 %gather_fusion.3 = f32[4096,128]{1,0:T(8,128)} fusion(f32[1024,128]{1,0:T(8,128)S(1)} %fusion.50, s32[4096]{0:T(1024)} %get-tuple-element.23), kind=kCustom, calls=%fused_computation.3 | custom fusion | bytes 4210688 | tf_op jit(solution)/shard_map/gather | solution.py:109
  320.1 3.9 fusion.98
  324.8 1.4 convolution_convert_fusion
  326.2 1.8 fusion.58
  328.0 1.8 fusion.62
  329.8 16.7 %all_gather.6 = bf16[1024,128]{1,0:T(8,128)(2,1)S(1)} all-gather(bf16[64,128]{1,0:T(8,128)(2,1)S(1)} %copy-done.22), channel_id=1, replica_groups=mesh['gx'=32,'gy'=16] {'gy'}, dimensions={0}, use_global_device_ids=true | all-gather | bytes 278528 | tf_op jit(solution)/shard_map/all_gather | solution.py:180
  346.5 1.6 fusion.11
  349.7 2.7 fusion.14
  354.7 22.8 %scatter_custom_fusion.4 = f32[1536,128]{1,0:T(8,128)S(1)} fusion(s32[4096]{0:T(1024)} %param.15, f32[4096,128]{1,0:T(8,128)} %fusion.58, f32[]{:T(128)} %constant.6.clone.1), kind=kCustom, calls=%fused_computation.61 | custom fusion | flops 524288 | bytes 786944 | tf_op jit(solution)/shard_map/scatter-add | solution.py:114
  377.5 22.8 %scatter_custom_fusion.3 = f32[1536,128]{1,0:T(8,128)S(1)} fusion(s32[4096]{0:T(1024)} %param.14, f32[4096,128]{1,0:T(8,128)} %fusion.62, f32[]{:T(128)} %constant.6.clone.1), kind=kCustom, calls=%fused_computation.63 | custom fusion | flops 524288 | bytes 786944 | tf_op jit(solution)/shard_map/scatter-add | solution.py:113
  400.5 1.3 fusion.9
  401.8 16.2 %collective-permute-start.4 = (bf16[1,128,128]{2,1,0:T(8,128)(2,1)S(1)}, bf16[1,128,128]{2,1,0:T(8,128)(2,1)S(1)}, u32[]{:S(2)}, u32[]{:S(2)}) collective-permute-start(bf16[1,128,128]{2,1,0:T(8,128)(2,1)S(1)} %get-tuple-element.11), channel_id=1, source_target_pairs={{0,16},{16,32},{32,48},{48,64},{64,80},{80,96},{96,112},{112,128},... | collective-permute-start | bytes 98312 | tf_op jit(solution)/shard_map/ppermute | solution.py:12
  418.1 1.3 collective-permute-start.7
  419.4 4.0 collective-permute-start.6
  423.4 2.1 collective-permute-start.5
  425.6 106.1 %psum.15 = f32[3,128]{1,0:T(4,128)} all-reduce(f32[3,128]{1,0:T(4,128)S(1)} %pad_maximum_fusion.6), channel_id=1, replica_groups=mesh['gx'=32,'gy'=16] {'gx','gy'}, use_global_device_ids=true, to_apply=%region_12.13 | all-reduce | flops 384 | bytes 3072 | tf_op jit(solution)/shard_map/psum | solution.py:220
  531.7 3.7 scatter_custom_fusion.5
  536.1 290.4 %all-reduce.2.cloned.1.call-done = f32[9,128,128]{2,1,0:T(8,128)} async-done(((f32[9,128,128]{2,1,0:T(8,128)}), f32[9,128,128]{2,1,0:T(8,128)}) %all-reduce.2.cloned.1.call-update) | async-done | bytes 589840 | tf_op jit(solution)/shard_map/psum | solution.py:220
  826.5 1.9 copy.36
  (99 shorter events, 13.1 us)
Async XLA Ops:
  7.2 25.7 %copy-start = (bf16[4096,128]{1,0:T(8,128)(2,1)S(1)}, bf16[4096,128]{1,0:T(8,128)(2,1)}, u32[]{:S(2)}) copy-start(bf16[4096,128]{1,0:T(8,128)(2,1)} %param.13) | copy-start | bytes 3145732
  7.2 24.7 %copy-start.1 = (bf16[1024,128]{1,0:T(8,128)(2,1)S(1)}, bf16[1024,128]{1,0:T(8,128)(2,1)}, u32[]{:S(2)}) copy-start(bf16[1024,128]{1,0:T(8,128)(2,1)} %param.12) | copy-start | bytes 786436
  7.2 25.6 %copy-start.14 = (bf16[4,128,128]{2,1,0:T(8,128)(2,1)S(1)}, bf16[4,128,128]{2,1,0:T(8,128)(2,1)}, u32[]{:S(2)}) copy-start(bf16[4,128,128]{2,1,0:T(8,128)(2,1)} %param.20) | copy-start | bytes 393220
  7.2 183.5 %reduce-scatter.3.cloned.1.call-start = ((), (), s32[]{:S(2)}) async-start(), calls=%async_computation.2 | async-start | bytes 557056 | tf_op jit(solution)/shard_map/reduce_scatter | solution.py:173
  10.1 25.2 %collective-permute-start.3 = (bf16[1,128,128]{2,1,0:T(8,128)(2,1)S(1)}, bf16[1,128,128]{2,1,0:T(8,128)(2,1)S(1)}, u32[]{:S(2)}, u32[]{:S(2)}) collective-permute-start(bf16[1,128,128]{2,1,0:T(8,128)(2,1)S(1)} %get-tuple-element.19), channel_id=1, source_target_pairs={{1,0},{2,1},{3,2},{4,3},{5,4},{6,5},{7,6},{8,7},{9,8},{10,9},{11,1... | collective-permute-start | bytes 98312 | tf_op jit(solution)/shard_map/ppermute | solution.py:15
  11.4 23.8 %collective-permute-start.2 = (bf16[1,128,128]{2,1,0:T(8,128)(2,1)S(1)}, bf16[1,128,128]{2,1,0:T(8,128)(2,1)S(1)}, u32[]{:S(2)}, u32[]{:S(2)}) collective-permute-start(bf16[1,128,128]{2,1,0:T(8,128)(2,1)S(1)} %get-tuple-element.20), channel_id=1, source_target_pairs={{0,1},{1,2},{2,3},{3,4},{4,5},{5,6},{6,7},{7,8},{8,9},{9,10},{10,1... | collective-permute-start | bytes 98312 | tf_op jit(solution)/shard_map/ppermute | solution.py:12
  16.0 19.2 %collective-permute-start.1 = (bf16[1,128,128]{2,1,0:T(8,128)(2,1)S(1)}, bf16[1,128,128]{2,1,0:T(8,128)(2,1)S(1)}, u32[]{:S(2)}, u32[]{:S(2)}) collective-permute-start(bf16[1,128,128]{2,1,0:T(8,128)(2,1)S(1)} %get-tuple-element.21), channel_id=1, source_target_pairs={{16,0},{32,16},{48,32},{64,48},{80,64},{96,80},{112,96},{128,112},... | collective-permute-start | bytes 98312 | tf_op jit(solution)/shard_map/ppermute | solution.py:15
  24.8 10.5 %collective-permute-start = (bf16[1,128,128]{2,1,0:T(8,128)(2,1)S(1)}, bf16[1,128,128]{2,1,0:T(8,128)(2,1)S(1)}, u32[]{:S(2)}, u32[]{:S(2)}) collective-permute-start(bf16[1,128,128]{2,1,0:T(8,128)(2,1)S(1)} %get-tuple-element.22), channel_id=1, source_target_pairs={{0,16},{16,32},{32,48},{48,64},{64,80},{80,96},{96,112},{112,128},... | collective-permute-start | bytes 98312 | tf_op jit(solution)/shard_map/ppermute | solution.py:12
  62.5 1.2 copy-start.2
  62.5 1.9 copy-start.4
  64.4 1.8 copy-start.23
  93.5 0.8 copy-start.11
  103.6 198.0 %copy-start.25 = (s32[1024]{0:T(1024)S(1)}, s32[1024]{0:T(1024)}, u32[]{:S(2)}) copy-start(s32[1024]{0:T(1024)} %param.17) | copy-start | bytes 12292
  103.6 178.9 %reduce-scatter.5.cloned.1.call-start = ((), (), s32[]{:S(2)}) async-start(), calls=%async_computation.3 | async-start | bytes 557056 | tf_op jit(solution)/shard_map/reduce_scatter | solution.py:181
  111.0 192.3 %copy-start.12 = (f32[1024,128]{1,0:T(8,128)S(1)}, f32[1024,128]{1,0:T(8,128)}, u32[]{:S(2)}) copy-start(f32[1024,128]{1,0:T(8,128)} %copy-done.11) | copy-start | bytes 1572868
  111.0 715.5 %all-reduce.2.cloned.1.call-start = ((), (), s32[]{:S(2)}) async-start(), calls=%async_computation.4 | async-start | bytes 1179648 | tf_op jit(solution)/shard_map/psum | solution.py:220
  191.7 0.6 copy-start.20
  282.4 20.9 %copy-start.16 = (bf16[3,128,128]{2,1,0:T(8,128)(2,1)S(1)}, bf16[3,128,128]{2,1,0:T(8,128)(2,1)}, u32[]{:S(2)}) copy-start(bf16[3,128,128]{2,1,0:T(8,128)(2,1)} %param.21) | copy-start | bytes 294916
  283.4 0.9 copy-start.18
  303.3 1.3 copy-start.9
  303.7 0.7 copy-start.5
  320.1 3.9 copy-start.3
  323.9 0.9 copy-start.15
  328.0 1.8 copy-start.22
  328.0 18.5 %copy-start.27 = (f32[1024,128]{1,0:T(8,128)S(1)}, f32[1024,128]{1,0:T(8,128)}, u32[]{:S(2)}) copy-start(f32[1024,128]{1,0:T(8,128)} %convolution_add_fusion.2) | copy-start | bytes 1572868
  348.1 1.6 copy-start.7
  348.1 1.6 copy-start.24
  349.7 2.7 copy-start.6
  349.7 3.3 copy-start.10
  349.7 3.4 copy-start.13
  352.5 1.0 copy-start.17
  352.5 1.0 copy-start.19
  352.5 1.2 copy-start.21
  352.5 1.1 copy-start.28
  353.8 0.8 copy-start.8
  400.4 25.1 %copy-start.26 = (f32[128]{0:T(128)S(1)}, f32[128]{0:T(128)}, u32[]{:S(2)}) copy-start(f32[128]{0:T(128)} %get-tuple-element.7) | copy-start | bytes 1540
  401.8 129.8 %collective-permute-start.4 = (bf16[1,128,128]{2,1,0:T(8,128)(2,1)S(1)}, bf16[1,128,128]{2,1,0:T(8,128)(2,1)S(1)}, u32[]{:S(2)}, u32[]{:S(2)}) collective-permute-start(bf16[1,128,128]{2,1,0:T(8,128)(2,1)S(1)} %get-tuple-element.11), channel_id=1, source_target_pairs={{0,16},{16,32},{32,48},{48,64},{64,80},{80,96},{96,112},{112,128},... | collective-permute-start | bytes 98312 | tf_op jit(solution)/shard_map/ppermute | solution.py:12
  418.1 113.5 %collective-permute-start.7 = (bf16[1,128,128]{2,1,0:T(8,128)(2,1)S(1)}, bf16[1,128,128]{2,1,0:T(8,128)(2,1)S(1)}, u32[]{:S(2)}, u32[]{:S(2)}) collective-permute-start(bf16[1,128,128]{2,1,0:T(8,128)(2,1)S(1)} %get-tuple-element.12), channel_id=1, source_target_pairs={{1,0},{2,1},{3,2},{4,3},{5,4},{6,5},{7,6},{8,7},{9,8},{10,9},{11,1... | collective-permute-start | bytes 98312 | tf_op jit(solution)/shard_map/ppermute | solution.py:15
  419.4 112.2 %collective-permute-start.6 = (bf16[1,128,128]{2,1,0:T(8,128)(2,1)S(1)}, bf16[1,128,128]{2,1,0:T(8,128)(2,1)S(1)}, u32[]{:S(2)}, u32[]{:S(2)}) collective-permute-start(bf16[1,128,128]{2,1,0:T(8,128)(2,1)S(1)} %get-tuple-element.13), channel_id=1, source_target_pairs={{0,1},{1,2},{2,3},{3,4},{4,5},{5,6},{6,7},{7,8},{8,9},{9,10},{10,1... | collective-permute-start | bytes 98312 | tf_op jit(solution)/shard_map/ppermute | solution.py:12
  423.4 108.3 %collective-permute-start.5 = (bf16[1,128,128]{2,1,0:T(8,128)(2,1)S(1)}, bf16[1,128,128]{2,1,0:T(8,128)(2,1)S(1)}, u32[]{:S(2)}, u32[]{:S(2)}) collective-permute-start(bf16[1,128,128]{2,1,0:T(8,128)(2,1)S(1)} %get-tuple-element.14), channel_id=1, source_target_pairs={{16,0},{32,16},{48,32},{64,48},{80,64},{96,80},{112,96},{128,112},... | collective-permute-start | bytes 98312 | tf_op jit(solution)/shard_map/ppermute | solution.py:15
Sparse Core Ops, SparseCore 0:
  103.7 87.0 reduce-scatter.2
  195.3 87.0 reduce-scatter.4
  354.8 471.6 all-reduce.1
where the time goes:
time: 837 us; the launch traced here: 835 us
  waiting for transfers between devices  459 us (55%)
  blocking collectives  140 us (17%)
  other arithmetic  91 us (11%)
  local copies, waits for them, and re-layouts  54.8 us (7%)
  starting transfers between devices  40.3 us (5%)
  matrix products  35.1 us (4%)
  between operations  14.9 us (2%)
    psum x1, waiting for transfers between devices, body(): lax.psum((weight_local, bias_local), ('gx', 'gy'))  290 us
    psum x1, blocking collectives, body(): lax.psum((weight_local, bias_local), ('gx', 'gy'))  106 us
    reduce_scatter x1, waiting for transfers between devices, body(): lax.psum_scatter(owner_sums(grad_out, owner, jnp.int32(0), owned * lax.ax...  88.7 us
    reduce_scatter x1, waiting for transfers between devices, body(): lax.psum_scatter(0.0625 * owner_sums(fine_state, owner, jnp.int32(0), own...  79.7 us
    ppermute x4, starting transfers between devices, padded(): lax.ppermute(lax.slice_in_dim(block, block.shape[dim] - width, None, axis...  26.7 us
    scatter-add x1, other arithmetic, edge_back(): jax.ops.segment_sum(right_t(d_pre_bf, w_edge[1]), receivers, num_segments...  22.8 us
    scatter-add x1, other arithmetic, edge_back(): jax.ops.segment_sum(right_t(d_pre_bf, w_edge[0]), senders, num_segments=e...  22.8 us
    scatter-add x1, other arithmetic, node_front(): jax.ops.segment_sum(message, receivers, num_segments=nodes.shape[0])  22.8 us
  transfers between devices with their start and end apart: 11, of which 3 were waited for; matrix products, arithmetic and copies ran while one was open for 8% of the time, Pallas kernels for 0%

commit v1 on v0

v1 whole, which is shorter than its diff:
```python
import functools

import jax
import jax.numpy as jnp
from jax import lax
from jax.experimental import pallas as pl
from jax.experimental.pallas import tpu as pltpu
from jax.sharding import PartitionSpec as P

F32, BF16, I32 = jnp.float32, jnp.bfloat16, jnp.int32
W = 128
BLOCK = 256
MESH = pl.DeviceIdType.MESH


def dot(left, right):
    return jnp.dot(left, right, preferred_element_type=F32)


def right_t(left, right):
    return lax.dot_general(left, right, (((1,), (1,)), ((), ())), preferred_element_type=F32)


def sigmoid(value):
    return 0.5 * jnp.tanh(0.5 * value) + 0.5


def slope(value, sigma):
    return sigma * (1.0 + value * (1.0 - sigma))


def lane_row(ref, first, count):
    return jnp.concatenate([ref[pl.ds(first + q, 1), :] for q in range(count)], axis=1)


def kernel(
    dims,
    nodes,
    feat,
    snd,
    rcv,
    slist,
    owner,
    live,
    cot,
    w_edge,
    w_node,
    w_coarse,
    bias,
    node_out,
    d_nodes,
    d_edges,
    grads,
    bias_grads,
    iota,
    ext_t,
    table_t,
    hot_list,
    own_t,
    own_n,
    pick,
    halo,
    slopes,
    h_acc,
    sr_acc,
    we_acc,
    fine,
    node_slope,
    d_part,
    hb,
    agg,
    hid,
    cot_src,
    cot_in,
    fine_src,
    fine_in,
    coarse_all,
    back_src,
    back_in,
    bias_rows,
    a_src,
    a_in,
    a_mine,
    a_pair,
    a_z,
    a_fin,
    a_all,
    b_flat,
    b_src,
    b_in,
    b_mine,
    b_pair,
    b_z,
    b_fin,
    b_all,
    halo_sem,
    back_sem,
    cot_sem,
    fine_sem,
    coarse_sem,
    a_rs_sem,
    a_pair_sem,
    a_z_sem,
    a_ag_sem,
    b_rs_sem,
    b_pair_sem,
    b_z_sem,
    b_ag_sem,
):
    nx, ny, cells, edges, tile = dims
    nz = nx // 2
    ext = cells + 4 * W
    owned = cells // ny
    i, j = lax.axis_index("gx"), lax.axis_index("gy")
    core, z = lax.rem(i, 2), lax.div(i, 2)
    up, down = lax.rem(i + nx - 1, nx), lax.rem(i + 1, nx)
    left, right = lax.rem(j + ny - 1, ny), lax.rem(j + 1, ny)
    partner = i + 1 - 2 * core

    barrier = pltpu.get_barrier_semaphore()

    def greet(gx, gy):
        pl.semaphore_signal(barrier, inc=1, device_id=(gx, gy), device_id_type=MESH)

    greet(up, j)
    greet(down, j)

    def greet_row(d, c):
        greet(i, lax.rem(j + d, ny))
        return c

    def greet_column(d, c):
        greet(lax.rem(i + 2 * d, nx), j)
        return c

    lax.fori_loop(1, ny, greet_row, 0)
    lax.fori_loop(1, nz, greet_column, 0)

    def row_copy(src, dst, sems, slot, target):
        return pltpu.make_async_remote_copy(
            src_ref=src,
            dst_ref=dst.at[slot],
            send_sem=sems.at[0, target],
            recv_sem=sems.at[1, slot],
            device_id=(i, target),
            device_id_type=MESH,
        )

    def scatter_start(src, dst, sems):
        dst[j] = src[j]

        def step(d, c):
            t = lax.rem(j + d, ny)
            row_copy(src.at[t], dst, sems, j, t).start()
            return c

        lax.fori_loop(1, ny, step, 0)

    def gather_start(buf, sems):
        def step(d, c):
            t = lax.rem(j + d, ny)
            row_copy(buf.at[j], buf, sems, j, t).start()
            return c

        lax.fori_loop(1, ny, step, 0)

    def row_arrive(buf, sems):
        def step(d, c):
            t = lax.rem(j + d, ny)
            row_copy(buf.at[t], buf, sems, t, t).wait_recv()
            return c

        lax.fori_loop(1, ny, step, 0)

    def row_sent(src, dst, sems):
        def step(d, c):
            t = lax.rem(j + d, ny)
            row_copy(src.at[j], dst, sems, j, t).wait_send()
            return c

        lax.fori_loop(1, ny, step, 0)

    def z_copy(buf, sems, slot, target):
        return pltpu.make_async_remote_copy(
            src_ref=buf.at[slot],
            dst_ref=buf.at[slot],
            send_sem=sems.at[0, target],
            recv_sem=sems.at[1, slot],
            device_id=(2 * target + core, j),
            device_id_type=MESH,
        )

    def z_each(action):
        def step(d, c):
            action(lax.rem(z + d, nz))
            return c

        lax.fori_loop(1, nz, step, 0)

    def pair_copy(src, dst, sems, which):
        return pltpu.make_async_remote_copy(
            src_ref=src,
            dst_ref=dst,
            send_sem=sems.at[0, which],
            recv_sem=sems.at[1, which],
            device_id=(partner, j),
            device_id_type=MESH,
        )

    def slots_sum(ref):
        def step(k, total):
            return total + ref[k].astype(F32)

        return lax.fori_loop(1, ref.shape[0], step, ref[0].astype(F32))

    def reduce_stages(src, into, mine, pair, zbuf, fin, everything, sems):
        rs_sem, pair_sem, z_sem, ag_sem = sems
        half = mine.shape[0] // 2
        here = pl.ds(pl.multiple_of(core * half, 8), half)
        there = pl.ds(pl.multiple_of((1 - core) * half, 8), half)
        first = pair_copy(mine.at[there], pair, pair_sem, 0)
        second = pair_copy(fin.at[here], fin.at[here], pair_sem, 1)
        second_in = pair_copy(fin.at[there], fin.at[there], pair_sem, 1)

        def start():
            scatter_start(src, into, rs_sem)

        def to_pair():
            row_arrive(into, rs_sem)
            mine[...] = slots_sum(into)
            first.start()

        def to_column():
            first.wait_recv()
            zbuf[z] = mine[here, :] + pair[...]
            z_each(lambda t: z_copy(zbuf, z_sem, z, t).start())

        def from_column():
            z_each(lambda t: z_copy(zbuf, z_sem, t, t).wait_recv())
            fin[here, :] = slots_sum(zbuf)
            second.start()

        def to_row():
            second_in.wait_recv()
            everything[j] = fin[...]
            gather_start(everything, ag_sem)

        def finish():
            row_arrive(everything, ag_sem)
            row_sent(src, into, rs_sem)
            first.wait_send()
            second.wait_send()
            z_each(lambda t: z_copy(zbuf, z_sem, z, t).wait_send())
            row_sent(everything, everything, ag_sem)

        return start, to_pair, to_column, from_column, to_row, finish

    a_stage = reduce_stages(
        a_src, a_in, a_mine, a_pair, a_z, a_fin, a_all, (a_rs_sem, a_pair_sem, a_z_sem, a_ag_sem)
    )
    b_stage = reduce_stages(
        b_src, b_in, b_mine, b_pair, b_z, b_fin, b_all, (b_rs_sem, b_pair_sem, b_z_sem, b_ag_sem)
    )

    def halo_copies(src, dst, sems):
        targets = ((up, j), (down, j), (i, left), (i, right))
        return [
            pltpu.make_async_remote_copy(
                src_ref=src.at[k],
                dst_ref=dst.at[k ^ 1],
                send_sem=sems.at[0, k],
                recv_sem=sems.at[1, k ^ 1],
                device_id=targets[k],
                device_id_type=MESH,
            )
            for k in range(4)
        ]

    present = (i > 0, i < nx - 1, j > 0, j < ny - 1)

    def hot(row, count):
        parts = []
        for a in range(count // BLOCK):
            inside = jnp.where(lax.shift_right_arithmetic(row, 8) == a, row & 255, -1)
            inside = inside.astype(F32).astype(BF16)
            same = iota[:, : row.shape[1]] == inside
            parts.append(jnp.where(same, jnp.ones((), BF16), jnp.zeros((), BF16)))
        return jnp.concatenate(parts, axis=0)

    eye = (
        lax.broadcasted_iota(I32, (W, W), 0) == lax.broadcasted_iota(I32, (W, W), 1)
    ).astype(F32).astype(BF16)

    def turned(block):
        return right_t(eye, block).astype(BF16)

    iota[...] = lax.broadcasted_iota(I32, iota.shape, 0).astype(F32).astype(BF16)
    ext_t[:, :cells] = turned(nodes[...])
    hot_list[...] = hot(lane_row(slist, 0, 4), cells)
    picked = dot(ext_t[:, :cells], hot_list[...]).astype(BF16)
    for k in range(4):
        pick[k] = picked[:, k * W : (k + 1) * W]

    pl.semaphore_wait(barrier, 2 + ny - 1 + nz - 1)
    halo_out = halo_copies(pick, halo, halo_sem)
    for copy in halo_out:
        copy.start()

    own_row = lane_row(owner, 0, cells // W)
    own_t[...] = hot(own_row, cells)
    cot_src[...] = dot(own_t[...], cot[...]).astype(BF16).reshape(ny, owned, W)
    scatter_start(cot_src, cot_in, cot_sem)

    ws_t, wr_t, we_t = [turned(w_edge[k]) for k in range(3)]
    b_col = jnp.broadcast_to(bias[0:1, :], (W, W)).T
    table_t[:, ext:] = dot(wr_t, ext_t[:, :cells]).astype(BF16)
    for copy in halo_out:
        copy.wait_recv()
    for k in range(4):
        ext_t[:, cells + k * W : cells + (k + 1) * W] = jnp.where(
            present[k], halo[k].astype(F32), 0.0
        ).astype(BF16)
    table_t[:, :ext] = (
        dot(ws_t, ext_t[...]) + jnp.concatenate([b_col] * (ext // W), axis=1)
    ).astype(BF16)

    h_acc[...] = jnp.zeros_like(h_acc)
    per = tile // W
    alive = live[0]

    def hot_senders(t):
        return hot(lane_row(snd, t * per, per), ext)

    def hot_receivers(t):
        place = t * tile + lax.broadcasted_iota(I32, (1, tile), 1)
        return hot(jnp.where(place < alive, lane_row(rcv, t * per, per), -1), cells)

    def feat_tile(t):
        return feat[pl.ds(pl.multiple_of(t * tile, tile), tile), :]

    def forward(t, c):
        mark_r = hot_receivers(t)
        pre = (
            dot(table_t[:, :ext], hot_senders(t))
            + dot(table_t[:, ext:], mark_r)
            + right_t(we_t, feat_tile(t))
        )
        sigma = sigmoid(pre)
        slopes[t] = slope(pre, sigma)
        h_acc[...] += right_t(mark_r, (pre * sigma).astype(BF16))
        return c

    lax.fori_loop(0, edges // tile, forward, 0)

    hb[...] = h_acc[...].astype(BF16)
    agg[...] = dot(hb[...], w_edge[3]).astype(BF16)
    pre_node = dot(nodes[...], w_node[0]) + dot(agg[...], w_node[1]) + bias[1:2, :]
    sigma = sigmoid(pre_node)
    node_slope[...] = slope(pre_node, sigma)
    hid[...] = (pre_node * sigma).astype(BF16)
    fine[...] = nodes[...].astype(F32) + dot(hid[...], w_node[2])
    fine_src[...] = dot(own_t[...], fine[...].astype(BF16)).astype(BF16).reshape(ny, owned, W)
    scatter_start(fine_src, fine_in, fine_sem)

    for q in range(cells // W):
        column = jnp.broadcast_to(owner[q : q + 1, :].astype(F32), (W, W)).T
        lanes = lax.broadcasted_iota(I32, (W, W), 1).astype(F32)
        own_n[q * W : (q + 1) * W, :] = jnp.concatenate(
            [
                jnp.where(column == lanes + float(k * W), 1.0, 0.0).astype(BF16)
                for k in range(cells // W)
            ],
            axis=1,
        )
    agg_t, hid_t, hb_t = turned(agg[...]), turned(hid[...]), turned(hb[...])

    row_arrive(cot_in, cot_sem)
    d_coarse = slots_sum(cot_in).astype(BF16)
    d_hidden = right_t(d_coarse, w_coarse[1])
    row_arrive(fine_in, fine_sem)
    coarse_bf = (0.0625 * slots_sum(fine_in)).astype(BF16)
    pre_coarse = dot(coarse_bf, w_coarse[0]) + bias[2:3, :]
    sigma = sigmoid(pre_coarse)
    coarse_hid = (pre_coarse * sigma).astype(BF16)
    d_pre_c = d_hidden * slope(pre_coarse, sigma)
    d_pre_c_bf = d_pre_c.astype(BF16)
    coarse_all[j] = jnp.concatenate(
        [dot(coarse_hid, w_coarse[1]).astype(BF16), right_t(d_pre_c_bf, w_coarse[0]).astype(BF16)],
        axis=1,
    )
    gather_start(coarse_all, coarse_sem)
    grad_rows = a_src.shape[1]
    g_v1 = dot(turned(coarse_bf), d_pre_c_bf)
    g_v2 = dot(turned(coarse_hid), d_coarse)
    bias_rows[...] = jnp.zeros_like(bias_rows)
    bias_rows[2:3, :] = jnp.sum(d_pre_c, axis=0, keepdims=True)
    row_arrive(coarse_all, coarse_sem)

    picked = dot(own_n[...], coarse_all[...].reshape(cells, 2 * W))
    node_out[...] = (fine[...] + picked[:, :W]).astype(BF16)
    d_fine = cot[...].astype(F32) + 0.0625 * picked[:, W:]
    d_fine_bf = d_fine.astype(BF16)
    d_pre_n = right_t(d_fine_bf, w_node[2]) * node_slope[...]
    d_pre_n_bf = d_pre_n.astype(BF16)
    bias_rows[1:2, :] = jnp.sum(d_pre_n, axis=0, keepdims=True)
    d_part[...] = d_fine + right_t(d_pre_n_bf, w_node[0])
    d_agg = right_t(d_pre_n_bf, w_node[1]).astype(BF16)
    table_t[:, ext:] = right_t(w_edge[3], d_agg).astype(BF16)
    a_src[...] = jnp.concatenate(
        [
            dot(hb_t, d_agg),
            dot(ext_t[:, :cells], d_pre_n_bf),
            dot(agg_t, d_pre_n_bf),
            dot(hid_t, d_fine_bf),
            g_v1,
            g_v2,
        ],
        axis=0,
    ).reshape(ny, grad_rows, W)
    a_stage[0]()

    sr_acc[...] = jnp.zeros_like(sr_acc)
    we_acc[...] = jnp.zeros_like(we_acc)

    def backward(t, c):
        mark_r = hot_receivers(t)
        d_pre = (dot(table_t[:, ext:], mark_r) * slopes[t]).astype(BF16)
        sr_acc[:ext, :] += right_t(hot_senders(t), d_pre)
        sr_acc[ext:, :] += right_t(mark_r, d_pre)
        we_acc[...] += dot(d_pre, feat_tile(t))
        d_edges[pl.ds(pl.multiple_of(t * tile, tile), tile), :] = (
            dot(w_edge[2], d_pre).T.astype(BF16)
        )
        return c

    tiles = edges // tile
    cuts = [tiles * k // 4 for k in range(5)]
    for k in range(4):
        lax.fori_loop(cuts[k], cuts[k + 1], backward, 0)
        a_stage[k + 1]()

    s_bf = sr_acc[:ext, :].astype(BF16)
    r_bf = sr_acc[ext:, :].astype(BF16)
    back_src[...] = right_t(s_bf[cells:, :], w_edge[0]).astype(BF16).reshape(4, W, W)
    back_out = halo_copies(back_src, back_in, back_sem)
    for copy in back_out:
        copy.start()
    bias_rows[0:1, :] = jnp.sum(sr_acc[ext:, :], axis=0, keepdims=True)
    b_flat[...] = jnp.concatenate(
        [dot(ext_t[...], s_bf), dot(ext_t[:, :cells], r_bf), we_acc[...].T], axis=0
    )
    share = b_flat.shape[0] // ny
    for k in range(ny):
        b_src[k, :share, :] = b_flat[k * share : (k + 1) * share, :]
        b_src[k, share:, :] = bias_rows[...]
    b_stage[0]()
    local = d_part[...] + right_t(s_bf[:cells, :], w_edge[0]) + right_t(r_bf, w_edge[1])
    for copy in back_out:
        copy.wait_recv()
    returned = jnp.concatenate(
        [jnp.where(present[k], back_in[k].astype(F32), 0.0) for k in range(4)], axis=0
    ).astype(BF16)
    d_nodes[...] = (local + dot(hot_list[...], returned)).astype(BF16)
    for stage in b_stage[1:5]:
        stage()
    a_stage[5]()
    grads[3 * W :, :] = a_all[...].reshape(6 * W, W)
    row_sent(cot_src, cot_in, cot_sem)
    row_sent(fine_src, fine_in, fine_sem)
    row_sent(coarse_all, coarse_all, coarse_sem)
    for copy in halo_out + back_out:
        copy.wait_send()
    b_stage[5]()
    for k in range(ny):
        grads[k * share : (k + 1) * share, :] = b_all[k, :share, :]
    bias_grads[...] = b_fin[share:, :]


def body(
    dims,
    nodes,
    edge_feat,
    senders,
    receivers,
    send_lists,
    owner,
    edge_live,
    cotangent,
    w_edge,
    w_node,
    w_coarse,
    biases,
):
    nx, ny, cells, edges, tile = dims
    nz = nx // 2
    ext = cells + 4 * W
    owned = cells // ny
    a_rows, b_rows = 6 * W // ny, 3 * W // ny + 8
    vmem = pl.BlockSpec(memory_space=pltpu.VMEM)
    smem = pl.BlockSpec(memory_space=pltpu.SMEM)

    def exchange(rows):
        return [
            pltpu.VMEM((ny, rows, W), F32),
            pltpu.VMEM((ny, rows, W), F32),
            pltpu.VMEM((rows, W), F32),
            pltpu.VMEM((rows // 2, W), F32),
            pltpu.VMEM((nz, rows // 2, W), F32),
            pltpu.VMEM((rows, W), F32),
            pltpu.VMEM((ny, rows, W), F32),
        ]

    b_exchange = exchange(b_rows)
    sems = [4, 4, ny, ny, ny] + [ny, 2, nz, ny] * 2
    outs = pl.pallas_call(
        functools.partial(kernel, dims),
        out_shape=(
            jax.ShapeDtypeStruct((cells, W), BF16),
            jax.ShapeDtypeStruct((cells, W), BF16),
            jax.ShapeDtypeStruct((edges, W), BF16),
            jax.ShapeDtypeStruct((9 * W, W), F32),
            jax.ShapeDtypeStruct((8, W), F32),
        ),
        in_specs=[vmem] * 6 + [smem] + [vmem] * 5,
        out_specs=(vmem,) * 5,
        scratch_shapes=[
            pltpu.VMEM((BLOCK, max(cells, tile)), BF16),
            pltpu.VMEM((W, ext), BF16),
            pltpu.VMEM((W, ext + cells), BF16),
            pltpu.VMEM((cells, 4 * W), BF16),
            pltpu.VMEM((cells, cells), BF16),
            pltpu.VMEM((cells, cells), BF16),
            pltpu.VMEM((4, W, W), BF16),
            pltpu.VMEM((4, W, W), BF16),
            pltpu.VMEM((edges // tile, W, tile), F32),
            pltpu.VMEM((cells, W), F32),
            pltpu.VMEM((ext + cells, W), F32),
            pltpu.VMEM((W, W), F32),
            pltpu.VMEM((cells, W), F32),
            pltpu.VMEM((cells, W), F32),
            pltpu.VMEM((cells, W), F32),
            pltpu.VMEM((cells, W), BF16),
            pltpu.VMEM((cells, W), BF16),
            pltpu.VMEM((cells, W), BF16),
            pltpu.VMEM((ny, owned, W), BF16),
            pltpu.VMEM((ny, owned, W), BF16),
            pltpu.VMEM((ny, owned, W), BF16),
            pltpu.VMEM((ny, owned, W), BF16),
            pltpu.VMEM((ny, owned, 2 * W), BF16),
            pltpu.VMEM((4, W, W), BF16),
            pltpu.VMEM((4, W, W), BF16),
            pltpu.VMEM((8, W), F32),
            *exchange(a_rows),
            pltpu.VMEM((3 * W, W), F32),
            *b_exchange,
        ]
        + [pltpu.SemaphoreType.DMA((2, count)) for count in sems],
        compiler_params=pltpu.CompilerParams(
            collective_id=0, has_side_effects=True, vmem_limit_bytes=48 * 1024 * 1024
        ),
        cost_estimate=pl.CostEstimate(
            flops=2 * edges * W * (2 * ext + 4 * cells + 4 * W),
            bytes_accessed=2 * W * (2 * edges + 4 * cells),
            transcendentals=edges * W,
        ),
        name="mesh_step",
    )(
        nodes,
        edge_feat,
        senders.reshape(edges // W, W),
        receivers.reshape(edges // W, W),
        send_lists.reshape(4, W),
        owner.reshape(cells // W, W),
        edge_live,
        cotangent,
        w_edge,
        w_node,
        w_coarse,
        biases,
    )
    node_out, d_nodes, d_edges, grads, bias_grads = outs
    return node_out, d_nodes, d_edges, grads.reshape(9, W, W), bias_grads[:3]


def solution(mesh, cells=1024, edges=4096, tile=512):
    both = ("gx", "gy")
    dims = (mesh.shape["gx"], mesh.shape["gy"], cells, edges, tile)
    in_specs = (
        P(both, None),
        P(both, None),
        P(both),
        P(both),
        P(both, None, None),
        P(both),
        P(both),
        P(both, None),
        P(),
        P(),
        P(),
        P(),
    )
    out_specs = (P(both, None), P(both, None), P(both, None), P(), P())
    return jax.shard_map(
        functools.partial(body, dims),
        mesh=mesh,
        in_specs=in_specs,
        out_specs=out_specs,
        check_vma=False,
    )
```

time: 837 us -> 114 us (0.14)
  waiting for transfers between devices: 459 us -> 0 us
  blocking collectives: 140 us -> 0 us
  Pallas kernels: 0 us -> 100 us
  other arithmetic: 91 us -> 0 us
  local copies, waits for them, and re-layouts: 54.8 us -> 11.6 us
  starting transfers between devices: 40.3 us -> 0 us
  matrix products: 35.1 us -> 0 us
  between operations: 14.9 us -> 1.35 us
    psum x1 -> x0, waiting for transfers between devices: 290 us -> none  [body(): lax.psum((weight_local, bias_local), ('gx', 'gy'))]
    reduce_scatter x2 -> x0, waiting for transfers between devices: 168 us -> none  [the longest x1 88.7 us: body(): lax.psum_scatter(owner_sums(grad_out, owner, jnp.int32(0), owned * lax.ax...]
    psum x1 -> x0, blocking collectives: 106 us -> none  [body(): lax.psum((weight_local, bias_local), ('gx', 'gy'))]
    pallas_call x0 -> x1, Pallas kernels: none -> 100 us  [body(): pl.pallas_call(functools.partial(kernel, dims), out_shape=(jax.ShapeDtype...]
    scatter-add x6 -> x0, other arithmetic: 85.1 us -> none  [the longest x1 22.8 us: edge_back(): jax.ops.segment_sum(right_t(d_pre_bf, w_edge[1]), receivers, num_segments...]
    gather x4 -> x0, local copies, waits for them, and re-layouts: 44.6 us -> none  [the longest x1 15.4 us: edge_back(): d_message = (d_agg[receivers] * live[:, None]).astype(jnp.bfloat16)]
    ppermute x8 -> x0, starting transfers between devices: 40.2 us -> none  [the longest x4 26.7 us: padded(): lax.ppermute(lax.slice_in_dim(block, block.shape[dim] - width, None, axis...]
    dot_general x29 -> x0, matrix products: 35.1 us -> none  [the longest x11 17.1 us: matmul(): return jnp.dot(left, right, preferred_element_type=jnp.float32)]
  transfers between devices with their start and end apart: 11 -> 0, of which waited for: 3 -> 0; matrix products, arithmetic and copies ran while one was open for 8% -> 0% of each run, Pallas kernels for 0% -> 0%
where the time goes in v1:
time: 114 us; the launch traced here: 113 us
  Pallas kernels  100 us (88%)
  local copies, waits for them, and re-layouts  11.6 us (10%)
  between operations  1.35 us (1%)
    pallas_call x1, Pallas kernels, body(): pl.pallas_call(functools.partial(kernel, dims), out_shape=(jax.ShapeDtype...  100 us
    unnamed x26, local copies, waits for them, and re-layouts  11.1 us

profile of v1, /device:TPU:1, one launch (start us, length us, event | category | flops | bytes accessed | tf_op | source)
XLA Modules:
  0.0 113.3 jit_solution(7100698982219907513)
XLA Ops:
  0.6 0.0 copy-start.10
  1.3 0.0 copy-start.8
  1.3 0.0 copy-start.9
  1.3 0.0 copy-done.10
  1.3 0.7 copy-done.8
  2.0 0.0 copy-done.9
  2.0 0.0 copy-start
  2.0 1.2 %copy-done = bf16[4096,128]{1,0:T(8,128)(2,1)S(1)} copy-done((bf16[4096,128]{1,0:T(8,128)(2,1)S(1)}, bf16[4096,128]{1,0:T(8,128)(2,1)}, u32[]{:S(2)}) %copy-start) | copy-done | bytes 1048600
  3.2 0.0 copy-start.1
  3.2 0.9 copy-done.1
  4.2 0.0 copy-start.2
  4.2 0.9 copy-done.2
  5.1 0.0 copy-start.3
  5.1 0.9 copy-done.3
  6.0 0.0 copy-start.4
  6.0 0.9 copy-done.4
  6.9 0.0 copy-start.5
  6.9 0.8 copy-done.5
  7.8 0.0 copy-start.6
  7.8 0.7 copy-done.6
  8.5 0.0 copy-start.7
  8.5 0.7 copy-done.7
  9.2 100.4 %mesh_step.1 = (bf16[1024,128]{1,0:T(8,128)(2,1)S(1)}, bf16[1024,128]{1,0:T(8,128)(2,1)S(1)}, bf16[4096,128]{1,0:T(8,128)(2,1)S(1)}, f32[1152,128]{1,0:T(8,128)S(1)}, f32[8,128]{1,0:T(8,128)S(1)}) custom-call(bf16[1024,128]{1,0:T(8,128)(2,1)S(1)} %copy-done.1, bf16[4096,128]{1,0:T(8,128)(2,1)S(1)} %copy-done, s32[32,128]{1,0:T(8,128)S(1)} %bitcast.6, ...), custom_call_target="tpu_custom_call" | custom-call | flops 8053063680 | bytes 3145728 | tf_op jit(solution)/shard_map/mesh_step/pallas_call | solution.py:515
  109.6 0.6 slice.3
  110.2 0.7 copy.22
  110.9 0.7 copy.23
  111.6 1.0 copy.24
  112.5 0.8 copy.25
Async XLA Ops:
  0.6 0.7 copy-start.10
  1.3 0.7 copy-start.8
  1.3 0.7 copy-start.9
  2.0 1.2 %copy-start = (bf16[4096,128]{1,0:T(8,128)(2,1)S(1)}, bf16[4096,128]{1,0:T(8,128)(2,1)}, u32[]{:S(2)}) copy-start(bf16[4096,128]{1,0:T(8,128)(2,1)} %feat.1) | copy-start | bytes 3145732
  3.2 0.9 copy-start.1
  4.2 0.9 copy-start.2
  5.1 0.9 copy-start.3
  6.0 0.9 copy-start.4
  6.9 0.8 copy-start.5
  7.8 0.7 copy-start.6
  8.5 0.7 copy-start.7

commit v2 on v0

v2 whole, which is shorter than its diff:
```python
import functools
from types import SimpleNamespace

import jax
import jax.numpy as jnp
from jax import lax
from jax.experimental import pallas as pl
from jax.experimental.pallas import tpu as pltpu
from jax.sharding import PartitionSpec as P

F32, BF16, I32 = jnp.float32, jnp.bfloat16, jnp.int32
W = 128
BLOCK = 256
MESH = pl.DeviceIdType.MESH


def dot(left, right):
    return jnp.dot(left, right, preferred_element_type=F32)


def right_t(left, right):
    return lax.dot_general(left, right, (((1,), (1,)), ((), ())), preferred_element_type=F32)


def sigmoid(value):
    return 0.5 * jnp.tanh(0.5 * value) + 0.5


def slope(value, sigma):
    return sigma * (1.0 + value * (1.0 - sigma))


def lane_row(ref, first, count):
    return jnp.concatenate([ref[pl.ds(first + q, 1), :] for q in range(count)], axis=1)


INPUTS = (
    "nodes", "feat", "snd", "rcv", "slist", "owner", "cot", "w_edge", "w_node", "w_coarse", "bias"
)
ORDER = (
    "slist", "nodes", "owner", "cot", "snd", "rcv", "w_edge", "bias", "feat", "w_node", "w_coarse"
)
OUTPUTS = ("node_out", "d_nodes", "d_edges", "grads", "bias_grads")


def kernel(dims, names, *refs):
    r = SimpleNamespace(**dict(zip(names, refs)))
    nx, ny, cells, edges, tile = dims
    nz = nx // 2
    ng = 2 * ny
    ext = cells + 4 * W
    owned = cells // ny
    tiles = edges // tile
    i, j = lax.axis_index("gx"), lax.axis_index("gy")
    core, z = lax.rem(i, 2), lax.div(i, 2)
    g = core * ny + j
    up, down = lax.rem(i + nx - 1, nx), lax.rem(i + 1, nx)
    left, right = lax.rem(j + ny - 1, ny), lax.rem(j + 1, ny)
    across = lax.rem(i + nx - 1 + 2 * core, nx)

    barrier = pltpu.get_barrier_semaphore()

    def greet(gx, gy):
        pl.semaphore_signal(barrier, inc=1, device_id=(gx, gy), device_id_type=MESH)

    def each(count, me, action):
        def step(d, c):
            action(lax.rem(me + d, count))
            return c

        lax.fori_loop(1, count, step, 0)

    greet(across, j)
    loads = {
        name: pltpu.make_async_copy(
            getattr(r, name + "_in"), getattr(r, name), r.load_sem.at[k]
        )
        for k, name in enumerate(ORDER)
    }
    for name in ORDER:
        loads[name].start()
    each(ng, g, lambda t: greet(2 * z + lax.div(t, ny), lax.rem(t, ny)))
    each(nz, z, lambda t: greet(2 * t + core, j))

    def exchange(count, me, place):
        def copy(src, dst, sems, slot, target):
            return pltpu.make_async_remote_copy(
                src_ref=src,
                dst_ref=dst.at[slot],
                send_sem=sems.at[0, target],
                recv_sem=sems.at[1, slot],
                device_id=place(target),
                device_id_type=MESH,
            )

        def scatter(src, dst, sems):
            dst[me] = src[me]
            each(count, me, lambda t: copy(src.at[t], dst, sems, me, t).start())

        def gather(buf, sems):
            each(count, me, lambda t: copy(buf.at[me], buf, sems, me, t).start())

        def arrive(buf, sems):
            each(count, me, lambda t: copy(buf.at[t], buf, sems, t, t).wait_recv())

        def sent(buf, sems):
            each(count, me, lambda t: copy(buf.at[me], buf, sems, me, t).wait_send())

        return SimpleNamespace(scatter=scatter, gather=gather, arrive=arrive, sent=sent)

    row = exchange(ny, j, lambda t: (i, t))
    column = exchange(nz, z, lambda t: (2 * t + core, j))
    layer = exchange(ng, g, lambda t: (2 * z + lax.div(t, ny), lax.rem(t, ny)))

    def slots_sum(ref):
        return jnp.sum(ref[...].astype(F32), axis=0)

    def reduce_stages(src, into, zbuf, everything, sums, sems):
        rs_sem, z_sem, ag_sem = sems

        def start():
            layer.scatter(src, into, rs_sem)

        def to_column():
            layer.arrive(into, rs_sem)
            zbuf[z] = slots_sum(into).astype(BF16)
            column.gather(zbuf, z_sem)

        def to_layer():
            column.arrive(zbuf, z_sem)
            sums[...] = slots_sum(zbuf)
            everything[g] = sums[...].astype(BF16)
            layer.gather(everything, ag_sem)

        def finish():
            layer.arrive(everything, ag_sem)

        def sent():
            layer.sent(into, rs_sem)
            column.sent(zbuf, z_sem)
            layer.sent(everything, ag_sem)

        return SimpleNamespace(
            start=start, to_column=to_column, to_layer=to_layer, finish=finish, sent=sent
        )

    a_stage = reduce_stages(
        r.a_src, r.a_in, r.a_z, r.a_all, r.a_sum, (r.a_rs_sem, r.a_z_sem, r.a_ag_sem)
    )
    b_stage = reduce_stages(
        r.b_src, r.b_in, r.b_z, r.b_all, r.b_sum, (r.b_rs_sem, r.b_z_sem, r.b_ag_sem)
    )

    def halo_copies(src, dst, sems):
        targets = ((up, j), (down, j), (i, left), (i, right))
        return [
            pltpu.make_async_remote_copy(
                src_ref=src.at[k],
                dst_ref=dst.at[k ^ 1],
                send_sem=sems.at[0, k],
                recv_sem=sems.at[1, k ^ 1],
                device_id=targets[k],
                device_id_type=MESH,
            )
            for k in range(4)
        ]

    present = (i > 0, i < nx - 1, j > 0, j < ny - 1)

    def hot(line, count):
        parts = []
        for a in range(count // BLOCK):
            inside = jnp.where(lax.shift_right_arithmetic(line, 8) == a, line & 255, -1)
            inside = inside.astype(F32).astype(BF16)
            same = r.iota[:, : line.shape[1]] == inside
            parts.append(jnp.where(same, jnp.ones((), BF16), jnp.zeros((), BF16)))
        return jnp.concatenate(parts, axis=0)

    eye = (
        lax.broadcasted_iota(I32, (W, W), 0) == lax.broadcasted_iota(I32, (W, W), 1)
    ).astype(F32).astype(BF16)

    def turned(block):
        return right_t(eye, block).astype(BF16)

    r.iota[...] = lax.broadcasted_iota(I32, r.iota.shape, 0).astype(F32).astype(BF16)
    loads["slist"].wait()
    r.hot_list[...] = hot(lane_row(r.slist, 0, 4), cells)
    loads["nodes"].wait()
    r.ext_t[:, :cells] = turned(r.nodes[...])
    picked = dot(r.ext_t[:, :cells], r.hot_list[...]).astype(BF16)
    for k in range(4):
        r.pick[k] = picked[:, k * W : (k + 1) * W]
    loads["owner"].wait()
    r.own_t[...] = hot(lane_row(r.owner, 0, cells // W), cells)
    loads["cot"].wait()
    r.cot_src[...] = dot(r.own_t[...], r.cot[...]).astype(BF16).reshape(ny, owned, W)

    pl.semaphore_wait(barrier, ng + nz - 1)
    halo_out = halo_copies(r.pick, r.halo, r.halo_sem)
    for copy in halo_out:
        copy.start()
    row.scatter(r.cot_src, r.cot_got, r.cot_sem)

    loads["snd"].wait()
    loads["rcv"].wait()
    per = tile // W
    alive = r.live[0]

    def mark(t, c):
        r.marks[t, :ext, :] = hot(lane_row(r.snd, t * per, per), ext)
        place = t * tile + lax.broadcasted_iota(I32, (1, tile), 1)
        line = jnp.where(place < alive, lane_row(r.rcv, t * per, per), -1)
        r.marks[t, ext:, :] = hot(line, cells)
        return c

    lax.fori_loop(0, tiles, mark, 0)

    loads["w_edge"].wait()
    loads["bias"].wait()
    ws_t, wr_t, we_t = [turned(r.w_edge[k]) for k in range(3)]
    b_col = jnp.broadcast_to(r.bias[0:1, :], (W, W)).T
    r.table_t[:, ext:] = dot(wr_t, r.ext_t[:, :cells]).astype(BF16)
    loads["feat"].wait()
    for copy in halo_out:
        copy.wait_recv()
    for k in range(4):
        r.ext_t[:, cells + k * W : cells + (k + 1) * W] = jnp.where(
            present[k], r.halo[k].astype(F32), 0.0
        ).astype(BF16)
    r.table_t[:, :ext] = (
        dot(ws_t, r.ext_t[...]) + jnp.concatenate([b_col] * (ext // W), axis=1)
    ).astype(BF16)

    r.h_acc[...] = jnp.zeros_like(r.h_acc)

    def edge_rows(t):
        return pl.ds(pl.multiple_of(t * tile, tile), tile)

    def forward(t, c):
        pre = dot(r.table_t[...], r.marks[t]) + right_t(we_t, r.feat[edge_rows(t), :])
        sigma = sigmoid(pre)
        r.slopes[t] = slope(pre, sigma)
        r.h_acc[...] += right_t(r.marks[t, ext:, :], (pre * sigma).astype(BF16))
        return c

    lax.fori_loop(0, tiles, forward, 0)

    loads["w_node"].wait()
    loads["w_coarse"].wait()
    r.hb[...] = r.h_acc[...].astype(BF16)
    r.agg[...] = dot(r.hb[...], r.w_edge[3]).astype(BF16)
    pre_node = dot(r.nodes[...], r.w_node[0]) + dot(r.agg[...], r.w_node[1]) + r.bias[1:2, :]
    sigma = sigmoid(pre_node)
    r.node_slope[...] = slope(pre_node, sigma)
    r.hid[...] = (pre_node * sigma).astype(BF16)
    r.fine[...] = r.nodes[...].astype(F32) + dot(r.hid[...], r.w_node[2])
    sums = dot(r.own_t[...], r.fine[...].astype(BF16))
    r.fine_src[...] = sums.astype(BF16).reshape(ny, owned, W)
    row.scatter(r.fine_src, r.fine_got, r.fine_sem)

    for q in range(cells // W):
        at = jnp.broadcast_to(r.owner[q : q + 1, :].astype(F32), (W, W)).T
        lanes = lax.broadcasted_iota(I32, (W, W), 1).astype(F32)
        r.own_n[q * W : (q + 1) * W, :] = jnp.concatenate(
            [
                jnp.where(at == lanes + float(k * W), 1.0, 0.0).astype(BF16)
                for k in range(cells // W)
            ],
            axis=1,
        )
    agg_t, hid_t, hb_t = turned(r.agg[...]), turned(r.hid[...]), turned(r.hb[...])

    row.arrive(r.cot_got, r.cot_sem)
    d_coarse = slots_sum(r.cot_got).astype(BF16)
    d_hidden = right_t(d_coarse, r.w_coarse[1])
    row.arrive(r.fine_got, r.fine_sem)
    coarse_bf = (0.0625 * slots_sum(r.fine_got)).astype(BF16)
    pre_coarse = dot(coarse_bf, r.w_coarse[0]) + r.bias[2:3, :]
    sigma = sigmoid(pre_coarse)
    coarse_hid = (pre_coarse * sigma).astype(BF16)
    d_pre_c = d_hidden * slope(pre_coarse, sigma)
    d_pre_c_bf = d_pre_c.astype(BF16)
    r.coarse_all[j] = jnp.concatenate(
        [
            dot(coarse_hid, r.w_coarse[1]).astype(BF16),
            right_t(d_pre_c_bf, r.w_coarse[0]).astype(BF16),
        ],
        axis=1,
    )
    row.gather(r.coarse_all, r.coarse_sem)
    g_v1 = dot(turned(coarse_bf), d_pre_c_bf)
    g_v2 = dot(turned(coarse_hid), d_coarse)
    b_own = r.b_src.shape[1]
    a_own = 6 * W // ng
    share = 3 * W // ng
    r.bias_rows[...] = jnp.zeros_like(r.bias_rows)
    r.bias_rows[share + 2 : share + 3, :] = jnp.sum(d_pre_c, axis=0, keepdims=True)
    row.arrive(r.coarse_all, r.coarse_sem)

    picked = dot(r.own_n[...], r.coarse_all[...].reshape(cells, 2 * W))
    r.node_out[...] = (r.fine[...] + picked[:, :W]).astype(BF16)
    d_fine = r.cot[...].astype(F32) + 0.0625 * picked[:, W:]
    d_fine_bf = d_fine.astype(BF16)
    d_pre_n = right_t(d_fine_bf, r.w_node[2]) * r.node_slope[...]
    d_pre_n_bf = d_pre_n.astype(BF16)
    r.bias_rows[share + 1 : share + 2, :] = jnp.sum(d_pre_n, axis=0, keepdims=True)
    r.d_part[...] = d_fine + right_t(d_pre_n_bf, r.w_node[0])
    d_agg = right_t(d_pre_n_bf, r.w_node[1]).astype(BF16)
    r.table_t[:, ext:] = right_t(r.w_edge[3], d_agg).astype(BF16)
    early = jnp.concatenate(
        [
            dot(hb_t, d_agg),
            dot(r.ext_t[:, :cells], d_pre_n_bf),
            dot(agg_t, d_pre_n_bf),
            dot(hid_t, d_fine_bf),
            g_v1,
            g_v2,
        ],
        axis=0,
    ).reshape(ng, a_own, W)
    spare = r.a_src.shape[1] - a_own
    if spare:
        early = jnp.concatenate([early, jnp.zeros((ng, spare, W), F32)], axis=1)
    r.a_src[...] = early.astype(BF16)
    a_stage.start()

    r.sr_acc[...] = jnp.zeros_like(r.sr_acc)
    r.we_acc[...] = jnp.zeros_like(r.we_acc)

    def backward(t, c):
        d_pre = (dot(r.table_t[:, ext:], r.marks[t, ext:, :]) * r.slopes[t]).astype(BF16)
        r.d_pre[t] = d_pre
        r.sr_acc[...] += right_t(r.marks[t], d_pre)
        r.we_acc[...] += dot(d_pre, r.feat[edge_rows(t), :])
        return c

    def edge_out(t, c):
        r.d_edges[edge_rows(t), :] = dot(r.w_edge[2], r.d_pre[t]).T.astype(BF16)
        return c

    half = tiles // 2
    lax.fori_loop(0, half, backward, 0)
    a_stage.to_column()
    lax.fori_loop(half, tiles, backward, 0)
    a_stage.to_layer()

    s_bf = r.sr_acc[:ext, :].astype(BF16)
    r_bf = r.sr_acc[ext:, :].astype(BF16)
    r.back_src[...] = right_t(s_bf[cells:, :], r.w_edge[0]).astype(BF16).reshape(4, W, W)
    back_out = halo_copies(r.back_src, r.back_got, r.back_sem)
    for copy in back_out:
        copy.start()
    r.bias_rows[share : share + 1, :] = jnp.sum(r.sr_acc[ext:, :], axis=0, keepdims=True)
    r.b_flat[: 3 * W, :] = jnp.concatenate(
        [dot(r.ext_t[...], s_bf), dot(r.ext_t[:, :cells], r_bf), r.we_acc[...].T], axis=0
    )
    r.b_flat[3 * W :, :] = jnp.zeros((b_own, W), F32)
    inner = lax.broadcasted_iota(I32, (b_own, W), 0) < share
    for k in range(ng):
        part = r.b_flat[k * share : k * share + b_own, :]
        r.b_src[k] = jnp.where(inner, part, r.bias_rows[...]).astype(BF16)
    b_stage.start()
    local = (
        r.d_part[...] + right_t(s_bf[:cells, :], r.w_edge[0]) + right_t(r_bf, r.w_edge[1])
    )
    r.d_part[...] = local
    lax.fori_loop(0, half, edge_out, 0)
    b_stage.to_column()
    for copy in back_out:
        copy.wait_recv()
    returned = jnp.concatenate(
        [jnp.where(present[k], r.back_got[k].astype(F32), 0.0) for k in range(4)], axis=0
    ).astype(BF16)
    r.d_nodes[...] = (r.d_part[...] + dot(r.hot_list[...], returned)).astype(BF16)
    lax.fori_loop(half, tiles, edge_out, 0)
    b_stage.to_layer()
    a_stage.finish()
    r.grads[3 * W :, :] = r.a_all[...].astype(F32)[:, :a_own, :].reshape(6 * W, W)
    row.sent(r.cot_got, r.cot_sem)
    row.sent(r.fine_got, r.fine_sem)
    row.sent(r.coarse_all, r.coarse_sem)
    for copy in halo_out + back_out:
        copy.wait_send()
    a_stage.sent()
    r.bias_grads[...] = r.b_sum[share : share + 3, :]
    b_stage.finish()
    for k in range(ng):
        r.grads[k * share : (k + 1) * share, :] = r.b_all[k].astype(F32)[:share, :]
    b_stage.sent()


def settle(*refs):
    count = len(OUTPUTS)
    sems = refs[2 * count]
    copies = [
        pltpu.make_async_copy(refs[k], refs[count + k], sems.at[k]) for k in range(count)
    ]
    for copy in copies:
        copy.start()
    for copy in copies:
        copy.wait()


def body(
    dims,
    nodes,
    edge_feat,
    senders,
    receivers,
    send_lists,
    owner,
    edge_live,
    cotangent,
    w_edge,
    w_node,
    w_coarse,
    biases,
):
    nx, ny, cells, edges, tile = dims
    nz = nx // 2
    ng = 2 * ny
    ext = cells + 4 * W
    owned = cells // ny
    a_rows = -(-(6 * W // ng) // 16) * 16
    b_rows = -(-(3 * W // ng + 3) // 16) * 16
    operands = dict(
        nodes=nodes,
        feat=edge_feat,
        snd=senders.reshape(edges // W, W),
        rcv=receivers.reshape(edges // W, W),
        slist=send_lists.reshape(4, W),
        owner=owner.reshape(cells // W, W),
        cot=cotangent,
        w_edge=w_edge,
        w_node=w_node,
        w_coarse=w_coarse,
        bias=biases,
    )
    scratch = {name: pltpu.VMEM(operands[name].shape, operands[name].dtype) for name in INPUTS}
    scratch |= dict(
        iota=pltpu.VMEM((BLOCK, max(cells, tile)), BF16),
        ext_t=pltpu.VMEM((W, ext), BF16),
        table_t=pltpu.VMEM((W, ext + cells), BF16),
        marks=pltpu.VMEM((edges // tile, ext + cells, tile), BF16),
        hot_list=pltpu.VMEM((cells, 4 * W), BF16),
        own_t=pltpu.VMEM((cells, cells), BF16),
        own_n=pltpu.VMEM((cells, cells), BF16),
        pick=pltpu.VMEM((4, W, W), BF16),
        halo=pltpu.VMEM((4, W, W), BF16),
        slopes=pltpu.VMEM((edges // tile, W, tile), F32),
        d_pre=pltpu.VMEM((edges // tile, W, tile), BF16),
        h_acc=pltpu.VMEM((cells, W), F32),
        sr_acc=pltpu.VMEM((ext + cells, W), F32),
        we_acc=pltpu.VMEM((W, W), F32),
        fine=pltpu.VMEM((cells, W), F32),
        node_slope=pltpu.VMEM((cells, W), F32),
        d_part=pltpu.VMEM((cells, W), F32),
        hb=pltpu.VMEM((cells, W), BF16),
        agg=pltpu.VMEM((cells, W), BF16),
        hid=pltpu.VMEM((cells, W), BF16),
        cot_src=pltpu.VMEM((ny, owned, W), BF16),
        cot_got=pltpu.VMEM((ny, owned, W), BF16),
        fine_src=pltpu.VMEM((ny, owned, W), BF16),
        fine_got=pltpu.VMEM((ny, owned, W), BF16),
        coarse_all=pltpu.VMEM((ny, owned, 2 * W), BF16),
        back_src=pltpu.VMEM((4, W, W), BF16),
        back_got=pltpu.VMEM((4, W, W), BF16),
        bias_rows=pltpu.VMEM((b_rows, W), F32),
        b_flat=pltpu.VMEM((3 * W + b_rows, W), F32),
        load_sem=pltpu.SemaphoreType.DMA((len(INPUTS),)),
        halo_sem=pltpu.SemaphoreType.DMA((2, 4)),
        back_sem=pltpu.SemaphoreType.DMA((2, 4)),
        cot_sem=pltpu.SemaphoreType.DMA((2, ny)),
        fine_sem=pltpu.SemaphoreType.DMA((2, ny)),
        coarse_sem=pltpu.SemaphoreType.DMA((2, ny)),
    )
    for name, rows in (("a", a_rows), ("b", b_rows)):
        scratch |= {
            name + "_src": pltpu.VMEM((ng, rows, W), BF16),
            name + "_in": pltpu.VMEM((ng, rows, W), BF16),
            name + "_z": pltpu.VMEM((nz, rows, W), BF16),
            name + "_all": pltpu.VMEM((ng, rows, W), BF16),
            name + "_sum": pltpu.VMEM((rows, W), F32),
            name + "_rs_sem": pltpu.SemaphoreType.DMA((2, ng)),
            name + "_z_sem": pltpu.SemaphoreType.DMA((2, nz)),
            name + "_ag_sem": pltpu.SemaphoreType.DMA((2, ng)),
        }
    names = tuple(name + "_in" for name in INPUTS) + ("live",) + OUTPUTS + tuple(scratch)
    vmem = pl.BlockSpec(memory_space=pltpu.VMEM)
    smem = pl.BlockSpec(memory_space=pltpu.SMEM)
    hbm = pl.BlockSpec(memory_space=pltpu.HBM)
    shapes = (
        jax.ShapeDtypeStruct((cells, W), BF16),
        jax.ShapeDtypeStruct((cells, W), BF16),
        jax.ShapeDtypeStruct((edges, W), BF16),
        jax.ShapeDtypeStruct((9 * W, W), F32),
        jax.ShapeDtypeStruct((3, W), F32),
    )
    outs = pl.pallas_call(
        functools.partial(kernel, dims, names),
        out_shape=shapes,
        in_specs=[hbm] * len(INPUTS) + [smem],
        out_specs=(vmem,) * 5,
        scratch_shapes=list(scratch.values()),
        compiler_params=pltpu.CompilerParams(
            collective_id=0, has_side_effects=True, vmem_limit_bytes=52 * 1024 * 1024
        ),
        cost_estimate=pl.CostEstimate(
            flops=2 * edges * W * (2 * ext + 4 * cells + 4 * W),
            bytes_accessed=2 * W * (2 * edges + 4 * cells),
            transcendentals=edges * W,
        ),
        name="mesh_step",
    )(*[operands[name] for name in INPUTS], edge_live)
    outs = pl.pallas_call(
        settle,
        out_shape=shapes,
        in_specs=[vmem] * 5,
        out_specs=(hbm,) * 5,
        scratch_shapes=[pltpu.SemaphoreType.DMA((5,))],
        name="settle",
    )(*outs)
    node_out, d_nodes, d_edges, grads, bias_grads = outs
    return node_out, d_nodes, d_edges, grads.reshape(9, W, W), bias_grads


def solution(mesh, cells=1024, edges=4096, tile=1024):
    both = ("gx", "gy")
    dims = (mesh.shape["gx"], mesh.shape["gy"], cells, edges, tile)
    in_specs = (
        P(both, None),
        P(both, None),
        P(both),
        P(both),
        P(both, None, None),
        P(both),
        P(both),
        P(both, None),
        P(),
        P(),
        P(),
        P(),
    )
    out_specs = (P(both, None), P(both, None), P(both, None), P(), P())
    return jax.shard_map(
        functools.partial(body, dims),
        mesh=mesh,
        in_specs=in_specs,
        out_specs=out_specs,
        check_vma=False,
    )
```

time: 837 us -> 104 us (0.12)
  waiting for transfers between devices: 459 us -> 0 us
  blocking collectives: 140 us -> 0 us
  Pallas kernels: 0 us -> 92.3 us
  other arithmetic: 91 us -> 0 us
  local copies, waits for them, and re-layouts: 54.8 us -> 9.48 us
  starting transfers between devices: 40.3 us -> 0 us
  matrix products: 35.1 us -> 0 us
  between operations: 14.9 us -> 1.35 us
    psum x1 -> x0, waiting for transfers between devices: 290 us -> none  [body(): lax.psum((weight_local, bias_local), ('gx', 'gy'))]
    reduce_scatter x2 -> x0, waiting for transfers between devices: 168 us -> none  [the longest x1 88.7 us: body(): lax.psum_scatter(owner_sums(grad_out, owner, jnp.int32(0), owned * lax.ax...]
    psum x1 -> x0, blocking collectives: 106 us -> none  [body(): lax.psum((weight_local, bias_local), ('gx', 'gy'))]
    pallas_call x0 -> x2, Pallas kernels: none -> 92.3 us  [the longest x1 89.4 us: body(): pl.pallas_call(functools.partial(kernel, dims, names), out_shape=shapes,...]
    scatter-add x6 -> x0, other arithmetic: 85.1 us -> none  [the longest x1 22.8 us: edge_back(): jax.ops.segment_sum(right_t(d_pre_bf, w_edge[1]), receivers, num_segments...]
    gather x4 -> x0, local copies, waits for them, and re-layouts: 44.6 us -> none  [the longest x1 15.4 us: edge_back(): d_message = (d_agg[receivers] * live[:, None]).astype(jnp.bfloat16)]
    ppermute x8 -> x0, starting transfers between devices: 40.2 us -> none  [the longest x4 26.7 us: padded(): lax.ppermute(lax.slice_in_dim(block, block.shape[dim] - width, None, axis...]
    dot_general x29 -> x0, matrix products: 35.1 us -> none  [the longest x11 17.1 us: matmul(): return jnp.dot(left, right, preferred_element_type=jnp.float32)]
  transfers between devices with their start and end apart: 11 -> 0, of which waited for: 3 -> 0; matrix products, arithmetic and copies ran while one was open for 8% -> 0% of each run, Pallas kernels for 0% -> 0%
where the time goes in v2:
time: 104 us; the launch traced here: 103 us
  Pallas kernels  92.3 us (89%)
  local copies, waits for them, and re-layouts  9.48 us (9%)
  between operations  1.35 us (1%)
    pallas_call x1, Pallas kernels, body(): pl.pallas_call(functools.partial(kernel, dims, names), out_shape=shapes,...  89.4 us
    unnamed x28, local copies, waits for them, and re-layouts  9.48 us
    pallas_call x1, Pallas kernels, body(): pl.pallas_call(settle, out_shape=shapes, in_specs=[vmem] * 5, out_specs=(...  2.95 us

profile of v2, /device:TPU:1, one launch (start us, length us, event | category | flops | bytes accessed | tf_op | source)
XLA Modules:
  0.0 103.1 jit_solution(18200008565649974489)
XLA Ops:
  0.6 0.0 copy-start.13
  1.3 0.0 copy-start.11
  1.3 0.0 copy-start.12
  1.3 0.0 copy-done.13
  1.3 0.7 copy-done.11
  2.0 0.0 copy-done.12
  2.0 0.0 copy-start.4
  2.0 0.9 copy-done.4
  3.0 0.0 copy-start.5
  3.0 0.9 copy-done.5
  3.9 0.0 copy-start.6
  3.9 0.9 copy-done.6
  4.8 0.0 copy-start.7
  4.8 0.9 copy-done.7
  5.7 0.0 copy-start.8
  5.7 0.8 copy-done.8
  6.5 0.0 copy-start.9
  6.5 0.7 copy-done.9
  7.3 0.0 copy-start.10
  7.3 0.7 copy-done.10
  8.0 89.4 %mesh_step.1 = (bf16[1024,128]{1,0:T(8,128)(2,1)S(1)}, bf16[1024,128]{1,0:T(8,128)(2,1)S(1)}, bf16[4096,128]{1,0:T(8,128)(2,1)}, f32[1152,128]{1,0:T(8,128)S(1)}, f32[3,128]{1,0:T(4,128)S(1)}) custom-call(bf16[1024,128]{1,0:T(8,128)(2,1)S(1)} %copy-done.4, bf16[4096,128]{1,0:T(8,128)(2,1)} %refs_1_.1, s32[32,128]{1,0:T(8,128)S(1)} %bitcast.5, ...), custom_call_target="tpu_custom_call" | custom-call | flops 8053063680 | bytes 3145728 | tf_op jit(solution)/shard_map/mesh_step/pallas_call | solution.py:500
  97.3 0.0 copy-start
  97.4 0.8 copy-done
  98.2 0.0 copy-start.1
  98.2 0.7 copy-done.1
  98.9 0.0 copy-start.2
  98.9 0.7 copy-done.2
  99.6 0.0 copy-start.3
  99.6 0.6 copy-done.3
  100.2 2.9 %settle.1 = (bf16[1024,128]{1,0:T(8,128)(2,1)}, bf16[1024,128]{1,0:T(8,128)(2,1)}, bf16[4096,128]{1,0:T(8,128)(2,1)}, f32[1152,128]{1,0:T(8,128)}, f32[3,128]{1,0:T(4,128)}) custom-call(bf16[1024,128]{1,0:T(8,128)(2,1)} %copy-done.1, bf16[1024,128]{1,0:T(8,128)(2,1)} %copy-done.2, bf16[4096,128]{1,0:T(8,128)(2,1)} %get-tuple-element.17.refs_2_, ...), custom_call_target="tpu_custom_call" | custom-call | tf_op jit(solution)/shard_map/settle/pallas_call | solution.py:516
Async XLA Ops:
  0.6 0.7 copy-start.13
  1.3 0.7 copy-start.11
  1.3 0.7 copy-start.12
  2.0 0.9 copy-start.4
  3.0 0.9 copy-start.5
  3.9 0.9 copy-start.6
  4.8 0.9 copy-start.7
  5.7 0.8 copy-start.8
  6.5 0.7 copy-start.9
  7.3 0.7 copy-start.10
  97.3 0.8 copy-start
  98.2 0.7 copy-start.1
  98.9 0.7 copy-start.2
  99.6 0.6 copy-start.3

commit v3 on v2

--- a/solution.py
+++ b/solution.py
@@ -167,6 +167,35 @@
 
     present = (i > 0, i < nx - 1, j > 0, j < ny - 1)
 
+    half_e, half_c = ext // 2, cells // 2
+
+    def folded(line, half):
+        return jnp.where(line >= half, line - half, line)
+
+    def pick_half(high, both):
+        return jnp.where(high, both[W:, :], both[:W, :])
+
+    def halves(high, value):
+        low = jnp.where(high, 0.0, value)
+        return jnp.concatenate([low, value - low], axis=0).astype(BF16)
+
+    def unfold(pairs):
+        return jnp.concatenate([pairs[:, :W], pairs[:, W:]], axis=0)
+
+    def fold_t(table, half):
+        return jnp.concatenate([table[:, :half], table[:, half:]], axis=0)
+
+    def to_coarse(value):
+        low = jnp.where(r.own_high[...] > 0.5, 0.0, value)
+        pairs = jnp.concatenate([low, value - low], axis=1).astype(BF16)
+        return unfold(dot(r.own_t[...], pairs)).astype(BF16).reshape(ny, owned, W)
+
+    def from_coarse(table):
+        flat = table.reshape(cells, W)
+        pairs = jnp.concatenate([flat[:half_c], flat[half_c:]], axis=1)
+        both = dot(r.own_n[...], pairs)
+        return jnp.where(r.own_high[...] > 0.5, both[:, W:], both[:, :W])
+
     def hot(line, count):
         parts = []
         for a in range(count // BLOCK):
@@ -192,9 +221,13 @@
     for k in range(4):
         r.pick[k] = picked[:, k * W : (k + 1) * W]
     loads["owner"].wait()
-    r.own_t[...] = hot(lane_row(r.owner, 0, cells // W), cells)
+    r.own_t[...] = hot(folded(lane_row(r.owner, 0, cells // W), half_c), half_c)
+    for q in range(cells // W):
+        at = jnp.broadcast_to(r.owner[q : q + 1, :].astype(F32), (W, W)).T
+        r.own_at[q * W : (q + 1) * W, :] = at
+    r.own_high[...] = jnp.where(r.own_at[...] >= float(half_c), 1.0, 0.0)
     loads["cot"].wait()
-    r.cot_src[...] = dot(r.own_t[...], r.cot[...]).astype(BF16).reshape(ny, owned, W)
+    r.cot_src[...] = to_coarse(r.cot[...].astype(F32))
 
     pl.semaphore_wait(barrier, ng + nz - 1)
     halo_out = halo_copies(r.pick, r.halo, r.halo_sem)
@@ -207,11 +240,22 @@
     per = tile // W
     alive = r.live[0]
 
+    def sender_row(t):
+        return lane_row(r.snd, t * per, per)
+
+    def receiver_row(t):
+        place = t * tile + lax.broadcasted_iota(I32, (1, tile), 1)
+        return jnp.where(place < alive, lane_row(r.rcv, t * per, per), -1)
+
+    def high_s(t):
+        return jnp.broadcast_to(sender_row(t), (W, tile)) >= half_e
+
+    def high_r(t):
+        return jnp.broadcast_to(receiver_row(t), (W, tile)) >= half_c
+
     def mark(t, c):
-        r.marks[t, :ext, :] = hot(lane_row(r.snd, t * per, per), ext)
-        place = t * tile + lax.broadcasted_iota(I32, (1, tile), 1)
-        line = jnp.where(place < alive, lane_row(r.rcv, t * per, per), -1)
-        r.marks[t, ext:, :] = hot(line, cells)
+        r.marks[t, :half_e, :] = hot(folded(sender_row(t), half_e), half_e)
+        r.marks[t, half_e:, :] = hot(folded(receiver_row(t), half_c), half_c)
         return c
 
     lax.fori_loop(0, tiles, mark, 0)
@@ -220,7 +264,7 @@
     loads["bias"].wait()
     ws_t, wr_t, we_t = [turned(r.w_edge[k]) for k in range(3)]
     b_col = jnp.broadcast_to(r.bias[0:1, :], (W, W)).T
-    r.table_t[:, ext:] = dot(wr_t, r.ext_t[:, :cells]).astype(BF16)
+    r.table_t[:, half_e:] = fold_t(dot(wr_t, r.ext_t[:, :cells]), half_c).astype(BF16)
     loads["feat"].wait()
     for copy in halo_out:
         copy.wait_recv()
@@ -228,8 +272,8 @@
         r.ext_t[:, cells + k * W : cells + (k + 1) * W] = jnp.where(
             present[k], r.halo[k].astype(F32), 0.0
         ).astype(BF16)
-    r.table_t[:, :ext] = (
-        dot(ws_t, r.ext_t[...]) + jnp.concatenate([b_col] * (ext // W), axis=1)
+    r.table_t[:, :half_e] = fold_t(
+        dot(ws_t, r.ext_t[...]) + jnp.concatenate([b_col] * (ext // W), axis=1), half_e
     ).astype(BF16)
 
     r.h_acc[...] = jnp.zeros_like(r.h_acc)
@@ -238,37 +282,37 @@
         return pl.ds(pl.multiple_of(t * tile, tile), tile)
 
     def forward(t, c):
-        pre = dot(r.table_t[...], r.marks[t]) + right_t(we_t, r.feat[edge_rows(t), :])
+        above = high_r(t)
+        pre = (
+            pick_half(high_s(t), dot(r.table_t[:, :half_e], r.marks[t, :half_e, :]))
+            + pick_half(above, dot(r.table_t[:, half_e:], r.marks[t, half_e:, :]))
+            + right_t(we_t, r.feat[edge_rows(t), :])
+        )
         sigma = sigmoid(pre)
         r.slopes[t] = slope(pre, sigma)
-        r.h_acc[...] += right_t(r.marks[t, ext:, :], (pre * sigma).astype(BF16))
+        r.h_acc[...] += right_t(r.marks[t, half_e:, :], halves(above, pre * sigma))
         return c
 
     lax.fori_loop(0, tiles, forward, 0)
 
     loads["w_node"].wait()
     loads["w_coarse"].wait()
-    r.hb[...] = r.h_acc[...].astype(BF16)
+    r.hb[...] = unfold(r.h_acc[...]).astype(BF16)
     r.agg[...] = dot(r.hb[...], r.w_edge[3]).astype(BF16)
     pre_node = dot(r.nodes[...], r.w_node[0]) + dot(r.agg[...], r.w_node[1]) + r.bias[1:2, :]
     sigma = sigmoid(pre_node)
     r.node_slope[...] = slope(pre_node, sigma)
     r.hid[...] = (pre_node * sigma).astype(BF16)
     r.fine[...] = r.nodes[...].astype(F32) + dot(r.hid[...], r.w_node[2])
-    sums = dot(r.own_t[...], r.fine[...].astype(BF16))
-    r.fine_src[...] = sums.astype(BF16).reshape(ny, owned, W)
+    r.fine_src[...] = to_coarse(r.fine[...])
     row.scatter(r.fine_src, r.fine_got, r.fine_sem)
 
-    for q in range(cells // W):
-        at = jnp.broadcast_to(r.owner[q : q + 1, :].astype(F32), (W, W)).T
-        lanes = lax.broadcasted_iota(I32, (W, W), 1).astype(F32)
-        r.own_n[q * W : (q + 1) * W, :] = jnp.concatenate(
-            [
-                jnp.where(at == lanes + float(k * W), 1.0, 0.0).astype(BF16)
-                for k in range(cells // W)
-            ],
-            axis=1,
-        )
+    lanes = lax.broadcasted_iota(I32, (cells, W), 1).astype(F32)
+    at = r.own_at[...] - float(half_c) * r.own_high[...]
+    r.own_n[...] = jnp.concatenate(
+        [jnp.where(at == lanes + float(k * W), 1.0, 0.0).astype(BF16) for k in range(half_c // W)],
+        axis=1,
+    )
     agg_t, hid_t, hb_t = turned(r.agg[...]), turned(r.hid[...]), turned(r.hb[...])
 
     row.arrive(r.cot_got, r.cot_sem)
@@ -281,13 +325,9 @@
     coarse_hid = (pre_coarse * sigma).astype(BF16)
     d_pre_c = d_hidden * slope(pre_coarse, sigma)
     d_pre_c_bf = d_pre_c.astype(BF16)
-    r.coarse_all[j] = jnp.concatenate(
-        [
-            dot(coarse_hid, r.w_coarse[1]).astype(BF16),
-            right_t(d_pre_c_bf, r.w_coarse[0]).astype(BF16),
-        ],
-        axis=1,
-    )
+    r.d_coarse_all[j] = right_t(d_pre_c_bf, r.w_coarse[0]).astype(BF16)
+    row.gather(r.d_coarse_all, r.d_coarse_sem)
+    r.coarse_all[j] = dot(coarse_hid, r.w_coarse[1]).astype(BF16)
     row.gather(r.coarse_all, r.coarse_sem)
     g_v1 = dot(turned(coarse_bf), d_pre_c_bf)
     g_v2 = dot(turned(coarse_hid), d_coarse)
@@ -296,18 +336,17 @@
     share = 3 * W // ng
     r.bias_rows[...] = jnp.zeros_like(r.bias_rows)
     r.bias_rows[share + 2 : share + 3, :] = jnp.sum(d_pre_c, axis=0, keepdims=True)
-    row.arrive(r.coarse_all, r.coarse_sem)
-
-    picked = dot(r.own_n[...], r.coarse_all[...].reshape(cells, 2 * W))
-    r.node_out[...] = (r.fine[...] + picked[:, :W]).astype(BF16)
-    d_fine = r.cot[...].astype(F32) + 0.0625 * picked[:, W:]
+    row.arrive(r.d_coarse_all, r.d_coarse_sem)
+
+    d_fine = r.cot[...].astype(F32) + 0.0625 * from_coarse(r.d_coarse_all[...])
     d_fine_bf = d_fine.astype(BF16)
     d_pre_n = right_t(d_fine_bf, r.w_node[2]) * r.node_slope[...]
     d_pre_n_bf = d_pre_n.astype(BF16)
     r.bias_rows[share + 1 : share + 2, :] = jnp.sum(d_pre_n, axis=0, keepdims=True)
-    r.d_part[...] = d_fine + right_t(d_pre_n_bf, r.w_node[0])
+    r.d_part[...] = d_fine
+    r.d_pre_n[...] = d_pre_n_bf
     d_agg = right_t(d_pre_n_bf, r.w_node[1]).astype(BF16)
-    r.table_t[:, ext:] = right_t(r.w_edge[3], d_agg).astype(BF16)
+    r.table_t[:, half_e:] = fold_t(right_t(r.w_edge[3], d_agg), half_c).astype(BF16)
     early = jnp.concatenate(
         [
             dot(hb_t, d_agg),
@@ -325,19 +364,30 @@
     r.a_src[...] = early.astype(BF16)
     a_stage.start()
 
-    r.sr_acc[...] = jnp.zeros_like(r.sr_acc)
+    r.s_acc[...] = jnp.zeros_like(r.s_acc)
+    r.r_acc[...] = jnp.zeros_like(r.r_acc)
     r.we_acc[...] = jnp.zeros_like(r.we_acc)
 
     def backward(t, c):
-        d_pre = (dot(r.table_t[:, ext:], r.marks[t, ext:, :]) * r.slopes[t]).astype(BF16)
-        r.d_pre[t] = d_pre
-        r.sr_acc[...] += right_t(r.marks[t], d_pre)
-        r.we_acc[...] += dot(d_pre, r.feat[edge_rows(t), :])
+        above = high_r(t)
+        got = pick_half(above, dot(r.table_t[:, half_e:], r.marks[t, half_e:, :]))
+        d_pre = got * r.slopes[t]
+        d_pre_bf = d_pre.astype(BF16)
+        r.d_pre[t] = d_pre_bf
+        r.s_acc[...] += right_t(r.marks[t, :half_e, :], halves(high_s(t), d_pre))
+        r.r_acc[...] += right_t(r.marks[t, half_e:, :], halves(above, d_pre))
+        r.we_acc[...] += dot(d_pre_bf, r.feat[edge_rows(t), :])
         return c
 
     def edge_out(t, c):
         r.d_edges[edge_rows(t), :] = dot(r.w_edge[2], r.d_pre[t]).T.astype(BF16)
         return c
+
+    leaving = []
+
+    def leave(k, src, dst):
+        leaving.append(pltpu.make_async_copy(src, dst, r.out_sem.at[k]))
+        leaving[-1].start()
 
     half = tiles // 2
     lax.fori_loop(0, half, backward, 0)
@@ -345,13 +395,14 @@
     lax.fori_loop(half, tiles, backward, 0)
     a_stage.to_layer()
 
-    s_bf = r.sr_acc[:ext, :].astype(BF16)
-    r_bf = r.sr_acc[ext:, :].astype(BF16)
+    s_bf = unfold(r.s_acc[...]).astype(BF16)
+    r_sum = unfold(r.r_acc[...])
+    r_bf = r_sum.astype(BF16)
     r.back_src[...] = right_t(s_bf[cells:, :], r.w_edge[0]).astype(BF16).reshape(4, W, W)
     back_out = halo_copies(r.back_src, r.back_got, r.back_sem)
     for copy in back_out:
         copy.start()
-    r.bias_rows[share : share + 1, :] = jnp.sum(r.sr_acc[ext:, :], axis=0, keepdims=True)
+    r.bias_rows[share : share + 1, :] = jnp.sum(r_sum, axis=0, keepdims=True)
     r.b_flat[: 3 * W, :] = jnp.concatenate(
         [dot(r.ext_t[...], s_bf), dot(r.ext_t[:, :cells], r_bf), r.we_acc[...].T], axis=0
     )
@@ -361,44 +412,48 @@
         part = r.b_flat[k * share : k * share + b_own, :]
         r.b_src[k] = jnp.where(inner, part, r.bias_rows[...]).astype(BF16)
     b_stage.start()
-    local = (
-        r.d_part[...] + right_t(s_bf[:cells, :], r.w_edge[0]) + right_t(r_bf, r.w_edge[1])
-    )
-    r.d_part[...] = local
-    lax.fori_loop(0, half, edge_out, 0)
-    b_stage.to_column()
+    r.d_part[...] = (
+        r.d_part[...]
+        + right_t(r.d_pre_n[...], r.w_node[0])
+        + right_t(s_bf[:cells, :], r.w_edge[0])
+        + right_t(r_bf, r.w_edge[1])
+    )
     for copy in back_out:
         copy.wait_recv()
     returned = jnp.concatenate(
         [jnp.where(present[k], r.back_got[k].astype(F32), 0.0) for k in range(4)], axis=0
     ).astype(BF16)
     r.d_nodes[...] = (r.d_part[...] + dot(r.hot_list[...], returned)).astype(BF16)
+    leave(0, r.d_nodes, r.d_nodes_out)
+    b_stage.to_column()
+    lax.fori_loop(0, half, edge_out, 0)
+    first, second = pl.ds(0, half * tile), pl.ds(half * tile, (tiles - half) * tile)
+    leave(1, r.d_edges.at[first], r.d_edges_out.at[first])
+    row.arrive(r.coarse_all, r.coarse_sem)
+    r.node_out[...] = (r.fine[...] + from_coarse(r.coarse_all[...])).astype(BF16)
+    leave(2, r.node_out, r.node_out_out)
+    b_stage.to_layer()
     lax.fori_loop(half, tiles, edge_out, 0)
-    b_stage.to_layer()
+    leave(3, r.d_edges.at[second], r.d_edges_out.at[second])
+    r.bias_grads[...] = r.b_sum[share : share + 3, :]
+    leave(4, r.bias_grads, r.bias_grads_out)
     a_stage.finish()
     r.grads[3 * W :, :] = r.a_all[...].astype(F32)[:, :a_own, :].reshape(6 * W, W)
+    late, soon = pl.ds(0, 3 * W), pl.ds(3 * W, 6 * W)
+    leave(5, r.grads.at[soon], r.grads_out.at[soon])
     row.sent(r.cot_got, r.cot_sem)
     row.sent(r.fine_got, r.fine_sem)
     row.sent(r.coarse_all, r.coarse_sem)
+    row.sent(r.d_coarse_all, r.d_coarse_sem)
     for copy in halo_out + back_out:
         copy.wait_send()
     a_stage.sent()
-    r.bias_grads[...] = r.b_sum[share : share + 3, :]
     b_stage.finish()
     for k in range(ng):
         r.grads[k * share : (k + 1) * share, :] = r.b_all[k].astype(F32)[:share, :]
+    leave(6, r.grads.at[late], r.grads_out.at[late])
     b_stage.sent()
-
-
-def settle(*refs):
-    count = len(OUTPUTS)
-    sems = refs[2 * count]
-    copies = [
-        pltpu.make_async_copy(refs[k], refs[count + k], sems.at[k]) for k in range(count)
-    ]
-    for copy in copies:
-        copy.start()
-    for copy in copies:
+    for copy in leaving:
         copy.wait()
 
 
@@ -437,21 +492,32 @@
         w_coarse=w_coarse,
         bias=biases,
     )
+    shapes = (
+        jax.ShapeDtypeStruct((cells, W), BF16),
+        jax.ShapeDtypeStruct((cells, W), BF16),
+        jax.ShapeDtypeStruct((edges, W), BF16),
+        jax.ShapeDtypeStruct((9 * W, W), F32),
+        jax.ShapeDtypeStruct((3, W), F32),
+    )
     scratch = {name: pltpu.VMEM(operands[name].shape, operands[name].dtype) for name in INPUTS}
+    scratch |= {name: pltpu.VMEM(s.shape, s.dtype) for name, s in zip(OUTPUTS, shapes)}
     scratch |= dict(
         iota=pltpu.VMEM((BLOCK, max(cells, tile)), BF16),
         ext_t=pltpu.VMEM((W, ext), BF16),
-        table_t=pltpu.VMEM((W, ext + cells), BF16),
-        marks=pltpu.VMEM((edges // tile, ext + cells, tile), BF16),
+        table_t=pltpu.VMEM((2 * W, (ext + cells) // 2), BF16),
+        marks=pltpu.VMEM((edges // tile, (ext + cells) // 2, tile), BF16),
         hot_list=pltpu.VMEM((cells, 4 * W), BF16),
-        own_t=pltpu.VMEM((cells, cells), BF16),
-        own_n=pltpu.VMEM((cells, cells), BF16),
+        own_t=pltpu.VMEM((cells // 2, cells), BF16),
+        own_n=pltpu.VMEM((cells, cells // 2), BF16),
+        own_at=pltpu.VMEM((cells, W), F32),
+        own_high=pltpu.VMEM((cells, W), F32),
         pick=pltpu.VMEM((4, W, W), BF16),
         halo=pltpu.VMEM((4, W, W), BF16),
         slopes=pltpu.VMEM((edges // tile, W, tile), F32),
         d_pre=pltpu.VMEM((edges // tile, W, tile), BF16),
-        h_acc=pltpu.VMEM((cells, W), F32),
-        sr_acc=pltpu.VMEM((ext + cells, W), F32),
+        h_acc=pltpu.VMEM((cells // 2, 2 * W), F32),
+        s_acc=pltpu.VMEM((ext // 2, 2 * W), F32),
+        r_acc=pltpu.VMEM((cells // 2, 2 * W), F32),
         we_acc=pltpu.VMEM((W, W), F32),
         fine=pltpu.VMEM((cells, W), F32),
         node_slope=pltpu.VMEM((cells, W), F32),
@@ -463,7 +529,9 @@
         cot_got=pltpu.VMEM((ny, owned, W), BF16),
         fine_src=pltpu.VMEM((ny, owned, W), BF16),
         fine_got=pltpu.VMEM((ny, owned, W), BF16),
-        coarse_all=pltpu.VMEM((ny, owned, 2 * W), BF16),
+        coarse_all=pltpu.VMEM((ny, owned, W), BF16),
+        d_coarse_all=pltpu.VMEM((ny, owned, W), BF16),
+        d_pre_n=pltpu.VMEM((cells, W), BF16),
         back_src=pltpu.VMEM((4, W, W), BF16),
         back_got=pltpu.VMEM((4, W, W), BF16),
         bias_rows=pltpu.VMEM((b_rows, W), F32),
@@ -474,6 +542,8 @@
         cot_sem=pltpu.SemaphoreType.DMA((2, ny)),
         fine_sem=pltpu.SemaphoreType.DMA((2, ny)),
         coarse_sem=pltpu.SemaphoreType.DMA((2, ny)),
+        d_coarse_sem=pltpu.SemaphoreType.DMA((2, ny)),
+        out_sem=pltpu.SemaphoreType.DMA((7,)),
     )
     for name, rows in (("a", a_rows), ("b", b_rows)):
         scratch |= {
@@ -486,25 +556,18 @@
             name + "_z_sem": pltpu.SemaphoreType.DMA((2, nz)),
             name + "_ag_sem": pltpu.SemaphoreType.DMA((2, ng)),
         }
-    names = tuple(name + "_in" for name in INPUTS) + ("live",) + OUTPUTS + tuple(scratch)
-    vmem = pl.BlockSpec(memory_space=pltpu.VMEM)
+    names = tuple(name + "_in" for name in INPUTS) + ("live",)
+    names += tuple(name + "_out" for name in OUTPUTS) + tuple(scratch)
     smem = pl.BlockSpec(memory_space=pltpu.SMEM)
     hbm = pl.BlockSpec(memory_space=pltpu.HBM)
-    shapes = (
-        jax.ShapeDtypeStruct((cells, W), BF16),
-        jax.ShapeDtypeStruct((cells, W), BF16),
-        jax.ShapeDtypeStruct((edges, W), BF16),
-        jax.ShapeDtypeStruct((9 * W, W), F32),
-        jax.ShapeDtypeStruct((3, W), F32),
-    )
     outs = pl.pallas_call(
         functools.partial(kernel, dims, names),
         out_shape=shapes,
         in_specs=[hbm] * len(INPUTS) + [smem],
-        out_specs=(vmem,) * 5,
+        out_specs=(hbm,) * 5,
         scratch_shapes=list(scratch.values()),
         compiler_params=pltpu.CompilerParams(
-            collective_id=0, has_side_effects=True, vmem_limit_bytes=52 * 1024 * 1024
+            collective_id=0, has_side_effects=True, vmem_limit_bytes=63 * 1024 * 1024
         ),
         cost_estimate=pl.CostEstimate(
             flops=2 * edges * W * (2 * ext + 4 * cells + 4 * W),
@@ -513,14 +576,6 @@
         ),
         name="mesh_step",
     )(*[operands[name] for name in INPUTS], edge_live)
-    outs = pl.pallas_call(
-        settle,
-        out_shape=shapes,
-        in_specs=[vmem] * 5,
-        out_specs=(hbm,) * 5,
-        scratch_shapes=[pltpu.SemaphoreType.DMA((5,))],
-        name="settle",
-    )(*outs)
     node_out, d_nodes, d_edges, grads, bias_grads = outs
     return node_out, d_nodes, d_edges, grads.reshape(9, W, W), bias_grads
 

time: 104 us -> 93.4 us (0.90)
  Pallas kernels: 92.3 us -> 85.6 us
  local copies, waits for them, and re-layouts: 9.48 us -> 6.27 us
    pallas_call x1, Pallas kernels: 89.4 us -> 85.6 us  [body(): pl.pallas_call(functools.partial(kernel, dims, names), out_shape=shapes,...]
    unnamed x28 -> x11, local copies, waits for them, and re-layouts: 9.48 us -> 6.27 us
    pallas_call x1 -> x0, Pallas kernels: 2.95 us -> none  [body(): pl.pallas_call(settle, out_shape=shapes, in_specs=[vmem] * 5, out_specs=(...]
where the time goes in v3:
time: 93.4 us; the launch traced here: 93.1 us
  Pallas kernels  85.6 us (92%)
  local copies, waits for them, and re-layouts  6.27 us (7%)
  between operations  1.3 us (1%)
    pallas_call x1, Pallas kernels, body(): pl.pallas_call(functools.partial(kernel, dims, names), out_shape=shapes,...  85.6 us
    unnamed x11, local copies, waits for them, and re-layouts  6.27 us

profile of v3, /device:TPU:1, one launch (start us, length us, event | category | flops | bytes accessed | tf_op | source)
XLA Modules:
  0.0 93.1 jit_solution(11312962764098265535)
XLA Ops:
  1.3 85.6 %mesh_step.1 = (bf16[1024,128]{1,0:T(8,128)(2,1)}, bf16[1024,128]{1,0:T(8,128)(2,1)}, bf16[4096,128]{1,0:T(8,128)(2,1)}, f32[1152,128]{1,0:T(8,128)}, f32[3,128]{1,0:T(4,128)}) custom-call(bf16[1024,128]{1,0:T(8,128)(2,1)} %refs_0_.1, bf16[4096,128]{1,0:T(8,128)(2,1)} %refs_1_.1, s32[32,128]{1,0:T(8,128)} %bitcast.6, s32[32,128]{1,0:T(8,128)} %bitcast.7, ...), custom_call_target="tpu_custom_call" | custom-call | flops 8053063680 | bytes 3145728 | tf_op jit(solution)/shard_map/mesh_step/pallas_call | solution.py:563
  86.9 0.0 copy-start
  86.9 1.8 %copy.23 = bf16[1024,128]{1,0:T(8,128)(2,1)} copy(bf16[1024,128]{1,0:T(8,128)(2,1)} %get-tuple-element.20) | data formatting | bytes 524288
  88.6 1.7 %copy.24 = bf16[1024,128]{1,0:T(8,128)(2,1)} copy(bf16[1024,128]{1,0:T(8,128)(2,1)} %get-tuple-element.21) | data formatting | bytes 524288
  90.3 0.0 copy-done
  90.3 0.0 copy-start.1
  90.3 1.0 %copy.25 = bf16[4096,128]{1,0:T(8,128)(2,1)} copy(bf16[4096,128]{1,0:T(8,128)(2,1)S(1)} %copy-done) | data formatting | bytes 2097152
  91.3 0.5 copy-done.1
  91.7 0.0 copy-start.2
  91.7 0.8 copy.26
  92.6 0.0 copy-done.2
  92.6 0.6 copy.27
Async XLA Ops:
  86.9 3.4 %copy-start = (bf16[4096,128]{1,0:T(8,128)(2,1)S(1)}, bf16[4096,128]{1,0:T(8,128)(2,1)}, u32[]{:S(2)}) copy-start(bf16[4096,128]{1,0:T(8,128)(2,1)} %get-tuple-element.22) | copy-start | bytes 3145732
  90.3 1.4 %copy-start.1 = (f32[1152,128]{1,0:T(8,128)S(1)}, f32[1152,128]{1,0:T(8,128)}, u32[]{:S(2)}) copy-start(f32[1152,128]{1,0:T(8,128)} %get-tuple-element.13) | copy-start | bytes 1769476
  91.7 0.8 copy-start.2

commit v4 on v3

--- a/solution.py
+++ b/solution.py
@@ -83,28 +83,32 @@
     each(nz, z, lambda t: greet(2 * t + core, j))
 
     def exchange(count, me, place):
-        def copy(src, dst, sems, slot, target):
+        def copy(src, dst, sems, target):
             return pltpu.make_async_remote_copy(
                 src_ref=src,
-                dst_ref=dst.at[slot],
-                send_sem=sems.at[0, target],
-                recv_sem=sems.at[1, slot],
+                dst_ref=dst,
+                send_sem=sems.at[0],
+                recv_sem=sems.at[1],
                 device_id=place(target),
                 device_id_type=MESH,
             )
 
         def scatter(src, dst, sems):
             dst[me] = src[me]
-            each(count, me, lambda t: copy(src.at[t], dst, sems, me, t).start())
+            each(count, me, lambda t: copy(src.at[t], dst.at[me], sems, t).start())
 
         def gather(buf, sems):
-            each(count, me, lambda t: copy(buf.at[me], buf, sems, me, t).start())
+            each(count, me, lambda t: copy(buf.at[me], buf.at[me], sems, t).start())
+
+        def every(buf, sems):
+            others = buf.at[pl.ds(0, count - 1)]
+            return copy(others, others, sems, lax.rem(me + 1, count))
 
         def arrive(buf, sems):
-            each(count, me, lambda t: copy(buf.at[t], buf, sems, t, t).wait_recv())
+            every(buf, sems).wait_recv()
 
         def sent(buf, sems):
-            each(count, me, lambda t: copy(buf.at[me], buf, sems, me, t).wait_send())
+            every(buf, sems).wait_send()
 
         return SimpleNamespace(scatter=scatter, gather=gather, arrive=arrive, sent=sent)
 
@@ -390,10 +394,9 @@
         leaving[-1].start()
 
     half = tiles // 2
-    lax.fori_loop(0, half, backward, 0)
+    lax.fori_loop(0, tiles - 1, backward, 0)
     a_stage.to_column()
-    lax.fori_loop(half, tiles, backward, 0)
-    a_stage.to_layer()
+    lax.fori_loop(tiles - 1, tiles, backward, 0)
 
     s_bf = unfold(r.s_acc[...]).astype(BF16)
     r_sum = unfold(r.r_acc[...])
@@ -412,6 +415,7 @@
         part = r.b_flat[k * share : k * share + b_own, :]
         r.b_src[k] = jnp.where(inner, part, r.bias_rows[...]).astype(BF16)
     b_stage.start()
+    a_stage.to_layer()
     r.d_part[...] = (
         r.d_part[...]
         + right_t(r.d_pre_n[...], r.w_node[0])
@@ -448,13 +452,39 @@
     for copy in halo_out + back_out:
         copy.wait_send()
     a_stage.sent()
+    layer.sent(r.b_in, r.b_rs_sem)
+    column.sent(r.b_z, r.b_z_sem)
     b_stage.finish()
     for k in range(ng):
         r.grads[k * share : (k + 1) * share, :] = r.b_all[k].astype(F32)[:share, :]
     leave(6, r.grads.at[late], r.grads_out.at[late])
-    b_stage.sent()
+    layer.sent(r.b_all, r.b_ag_sem)
     for copy in leaving:
         copy.wait()
+
+
+def settle(cuts, *refs):
+    count = len(cuts)
+    held, sems = refs[2 * count : 3 * count], refs[3 * count]
+    pieces = []
+    for k, parts in enumerate(cuts):
+        rows = refs[k].shape[0] // parts
+        pieces += [(k, pl.ds(p * rows, rows)) for p in range(parts)]
+    gets = [
+        pltpu.make_async_copy(refs[k].at[here], held[k].at[here], sems.at[0, n])
+        for n, (k, here) in enumerate(pieces)
+    ]
+    puts = [
+        pltpu.make_async_copy(held[k].at[here], refs[count + k].at[here], sems.at[1, n])
+        for n, (k, here) in enumerate(pieces)
+    ]
+    for get in gets:
+        get.start()
+    for get, put in zip(gets, puts):
+        get.wait()
+        put.start()
+    for put in puts:
+        put.wait()
 
 
 def body(
@@ -539,10 +569,10 @@
         load_sem=pltpu.SemaphoreType.DMA((len(INPUTS),)),
         halo_sem=pltpu.SemaphoreType.DMA((2, 4)),
         back_sem=pltpu.SemaphoreType.DMA((2, 4)),
-        cot_sem=pltpu.SemaphoreType.DMA((2, ny)),
-        fine_sem=pltpu.SemaphoreType.DMA((2, ny)),
-        coarse_sem=pltpu.SemaphoreType.DMA((2, ny)),
-        d_coarse_sem=pltpu.SemaphoreType.DMA((2, ny)),
+        cot_sem=pltpu.SemaphoreType.DMA((2,)),
+        fine_sem=pltpu.SemaphoreType.DMA((2,)),
+        coarse_sem=pltpu.SemaphoreType.DMA((2,)),
+        d_coarse_sem=pltpu.SemaphoreType.DMA((2,)),
         out_sem=pltpu.SemaphoreType.DMA((7,)),
     )
     for name, rows in (("a", a_rows), ("b", b_rows)):
@@ -552,9 +582,9 @@
             name + "_z": pltpu.VMEM((nz, rows, W), BF16),
             name + "_all": pltpu.VMEM((ng, rows, W), BF16),
             name + "_sum": pltpu.VMEM((rows, W), F32),
-            name + "_rs_sem": pltpu.SemaphoreType.DMA((2, ng)),
-            name + "_z_sem": pltpu.SemaphoreType.DMA((2, nz)),
-            name + "_ag_sem": pltpu.SemaphoreType.DMA((2, ng)),
+            name + "_rs_sem": pltpu.SemaphoreType.DMA((2,)),
+            name + "_z_sem": pltpu.SemaphoreType.DMA((2,)),
+            name + "_ag_sem": pltpu.SemaphoreType.DMA((2,)),
         }
     names = tuple(name + "_in" for name in INPUTS) + ("live",)
     names += tuple(name + "_out" for name in OUTPUTS) + tuple(scratch)
@@ -567,7 +597,7 @@
         out_specs=(hbm,) * 5,
         scratch_shapes=list(scratch.values()),
         compiler_params=pltpu.CompilerParams(
-            collective_id=0, has_side_effects=True, vmem_limit_bytes=63 * 1024 * 1024
+            collective_id=0, has_side_effects=True, vmem_limit_bytes=61440 * 1024
         ),
         cost_estimate=pl.CostEstimate(
             flops=2 * edges * W * (2 * ext + 4 * cells + 4 * W),
@@ -576,6 +606,17 @@
         ),
         name="mesh_step",
     )(*[operands[name] for name in INPUTS], edge_live)
+    cuts = (1, 1, 4, 2, 1)
+    outs = pl.pallas_call(
+        functools.partial(settle, cuts),
+        out_shape=shapes,
+        in_specs=[hbm] * 5,
+        out_specs=(hbm,) * 5,
+        scratch_shapes=[pltpu.VMEM(s.shape, s.dtype) for s in shapes]
+        + [pltpu.SemaphoreType.DMA((2, sum(cuts)))],
+        compiler_params=pltpu.CompilerParams(vmem_limit_bytes=60 * 1024 * 1024),
+        name="settle",
+    )(*outs)
     node_out, d_nodes, d_edges, grads, bias_grads = outs
     return node_out, d_nodes, d_edges, grads.reshape(9, W, W), bias_grads
 

time: 93.4 us -> 81.2 us (0.87)
  local copies, waits for them, and re-layouts: 6.27 us -> 0 us
  Pallas kernels: 85.6 us -> 79.7 us
    pallas_call x1, Pallas kernels: 85.6 us -> 77.3 us  [body(): pl.pallas_call(functools.partial(kernel, dims, names), out_shape=shapes,...]
    unnamed x11 -> x0, local copies, waits for them, and re-layouts: 6.27 us -> none
    pallas_call x0 -> x1, Pallas kernels: none -> 2.44 us  [body(): pl.pallas_call(functools.partial(settle, cuts), out_shape=shapes, in_spec...]
where the time goes in v4:
time: 81.2 us; the launch traced here: 81 us
  Pallas kernels  79.7 us (98%)
  between operations  1.29 us (2%)
    pallas_call x1, Pallas kernels, body(): pl.pallas_call(functools.partial(kernel, dims, names), out_shape=shapes,...  77.3 us
    pallas_call x1, Pallas kernels, body(): pl.pallas_call(functools.partial(settle, cuts), out_shape=shapes, in_spec...  2.44 us

profile of v4, /device:TPU:1, one launch (start us, length us, event | category | flops | bytes accessed | tf_op | source)
XLA Modules:
  0.0 81.0 jit_solution(12189022394284314263)
XLA Ops:
  1.3 77.3 %mesh_step.1 = (bf16[1024,128]{1,0:T(8,128)(2,1)}, bf16[1024,128]{1,0:T(8,128)(2,1)}, bf16[4096,128]{1,0:T(8,128)(2,1)}, f32[1152,128]{1,0:T(8,128)}, f32[3,128]{1,0:T(4,128)}) custom-call(bf16[1024,128]{1,0:T(8,128)(2,1)} %refs_0_.1, bf16[4096,128]{1,0:T(8,128)(2,1)} %refs_1_.1, s32[32,128]{1,0:T(8,128)} %bitcast.6, s32[32,128]{1,0:T(8,128)} %bitcast.7, ...), custom_call_target="tpu_custom_call" | custom-call | flops 8053063680 | bytes 3145728 | tf_op jit(solution)/shard_map/mesh_step/pallas_call | solution.py:593
  78.6 2.4 %settle.1 = (bf16[1024,128]{1,0:T(8,128)(2,1)}, bf16[1024,128]{1,0:T(8,128)(2,1)}, bf16[4096,128]{1,0:T(8,128)(2,1)}, f32[1152,128]{1,0:T(8,128)}, f32[3,128]{1,0:T(4,128)}) custom-call(bf16[1024,128]{1,0:T(8,128)(2,1)} %get-tuple-element.15.refs_0_, bf16[1024,128]{1,0:T(8,128)(2,1)} %get-tuple-element.16.refs_1_, ...), custom_call_target="tpu_custom_call" | custom-call | tf_op jit(solution)/shard_map/settle/pallas_call | solution.py:610

commit v5 on v4

--- a/solution.py
+++ b/solution.py
@@ -64,11 +64,22 @@
         pl.semaphore_signal(barrier, inc=1, device_id=(gx, gy), device_id_type=MESH)
 
     def each(count, me, action):
-        def step(d, c):
-            action(lax.rem(me + d, count))
+        some = 5 if count > 5 else 1
+        first = 1 + (count - 1) % some
+        for d in range(1, first):
+            action(me ^ d)
+
+        def step(k, c):
+            for u in range(some):
+                action(me ^ (first + k * some + u))
             return c
 
-        lax.fori_loop(1, count, step, 0)
+        lax.fori_loop(0, (count - first) // some, step, 0)
+
+    shift = ny.bit_length() - 1
+
+    def layer_place(t):
+        return 2 * z + lax.shift_right_logical(t, shift), t & (ny - 1)
 
     greet(across, j)
     loads = {
@@ -79,7 +90,7 @@
     }
     for name in ORDER:
         loads[name].start()
-    each(ng, g, lambda t: greet(2 * z + lax.div(t, ny), lax.rem(t, ny)))
+    each(ng, g, lambda t: greet(*layer_place(t)))
     each(nz, z, lambda t: greet(2 * t + core, j))
 
     def exchange(count, me, place):
@@ -102,7 +113,7 @@
 
         def every(buf, sems):
             others = buf.at[pl.ds(0, count - 1)]
-            return copy(others, others, sems, lax.rem(me + 1, count))
+            return copy(others, others, sems, me ^ 1)
 
         def arrive(buf, sems):
             every(buf, sems).wait_recv()
@@ -114,7 +125,7 @@
 
     row = exchange(ny, j, lambda t: (i, t))
     column = exchange(nz, z, lambda t: (2 * t + core, j))
-    layer = exchange(ng, g, lambda t: (2 * z + lax.div(t, ny), lax.rem(t, ny)))
+    layer = exchange(ng, g, layer_place)
 
     def slots_sum(ref):
         return jnp.sum(ref[...].astype(F32), axis=0)
@@ -297,7 +308,7 @@
         r.h_acc[...] += right_t(r.marks[t, half_e:, :], halves(above, pre * sigma))
         return c
 
-    lax.fori_loop(0, tiles, forward, 0)
+    lax.fori_loop(0, tiles, forward, 0, unroll=2)
 
     loads["w_node"].wait()
     loads["w_coarse"].wait()
@@ -394,9 +405,8 @@
         leaving[-1].start()
 
     half = tiles // 2
-    lax.fori_loop(0, tiles - 1, backward, 0)
+    lax.fori_loop(0, tiles, backward, 0, unroll=2)
     a_stage.to_column()
-    lax.fori_loop(tiles - 1, tiles, backward, 0)
 
     s_bf = unfold(r.s_acc[...]).astype(BF16)
     r_sum = unfold(r.r_acc[...])
@@ -415,7 +425,6 @@
         part = r.b_flat[k * share : k * share + b_own, :]
         r.b_src[k] = jnp.where(inner, part, r.bias_rows[...]).astype(BF16)
     b_stage.start()
-    a_stage.to_layer()
     r.d_part[...] = (
         r.d_part[...]
         + right_t(r.d_pre_n[...], r.w_node[0])
@@ -430,6 +439,7 @@
     r.d_nodes[...] = (r.d_part[...] + dot(r.hot_list[...], returned)).astype(BF16)
     leave(0, r.d_nodes, r.d_nodes_out)
     b_stage.to_column()
+    a_stage.to_layer()
     lax.fori_loop(0, half, edge_out, 0)
     first, second = pl.ds(0, half * tile), pl.ds(half * tile, (tiles - half) * tile)
     leave(1, r.d_edges.at[first], r.d_edges_out.at[first])

time: 81.2 us -> 76.5 us (0.942)
  Pallas kernels: 79.7 us -> 75.1 us
    pallas_call x1, Pallas kernels: 77.3 us -> 72.6 us  [body(): pl.pallas_call(functools.partial(kernel, dims, names), out_shape=shapes,...]
where the time goes in v5:
time: 76.5 us; the launch traced here: 76.4 us
  Pallas kernels  75.1 us (98%)
  between operations  1.29 us (2%)
    pallas_call x1, Pallas kernels, body(): pl.pallas_call(functools.partial(kernel, dims, names), out_shape=shapes,...  72.6 us
    pallas_call x1, Pallas kernels, body(): pl.pallas_call(functools.partial(settle, cuts), out_shape=shapes, in_spec...  2.44 us

profile of v5, /device:TPU:1, one launch (start us, length us, event | category | flops | bytes accessed | tf_op | source)
XLA Modules:
  0.0 76.4 jit_solution(15846464111168490766)
XLA Ops:
  1.3 72.6 %mesh_step.1 = (bf16[1024,128]{1,0:T(8,128)(2,1)}, bf16[1024,128]{1,0:T(8,128)(2,1)}, bf16[4096,128]{1,0:T(8,128)(2,1)}, f32[1152,128]{1,0:T(8,128)}, f32[3,128]{1,0:T(4,128)}) custom-call(bf16[1024,128]{1,0:T(8,128)(2,1)} %refs_0_.1, bf16[4096,128]{1,0:T(8,128)(2,1)} %refs_1_.1, s32[32,128]{1,0:T(8,128)} %bitcast.6, s32[32,128]{1,0:T(8,128)} %bitcast.7, ...), custom_call_target="tpu_custom_call" | custom-call | flops 8053063680 | bytes 3145728 | tf_op jit(solution)/shard_map/mesh_step/pallas_call | solution.py:603
  73.9 2.4 %settle.1 = (bf16[1024,128]{1,0:T(8,128)(2,1)}, bf16[1024,128]{1,0:T(8,128)(2,1)}, bf16[4096,128]{1,0:T(8,128)(2,1)}, f32[1152,128]{1,0:T(8,128)}, f32[3,128]{1,0:T(4,128)}) custom-call(bf16[1024,128]{1,0:T(8,128)(2,1)} %get-tuple-element.15.refs_0_, bf16[1024,128]{1,0:T(8,128)(2,1)} %get-tuple-element.16.refs_1_, ...), custom_call_target="tpu_custom_call" | custom-call | tf_op jit(solution)/shard_map/settle/pallas_call | solution.py:620

commit v6 on v5

--- a/solution.py
+++ b/solution.py
@@ -64,17 +64,8 @@
         pl.semaphore_signal(barrier, inc=1, device_id=(gx, gy), device_id_type=MESH)
 
     def each(count, me, action):
-        some = 5 if count > 5 else 1
-        first = 1 + (count - 1) % some
-        for d in range(1, first):
+        for d in range(1, count):
             action(me ^ d)
-
-        def step(k, c):
-            for u in range(some):
-                action(me ^ (first + k * some + u))
-            return c
-
-        lax.fori_loop(0, (count - first) // some, step, 0)
 
     shift = ny.bit_length() - 1
 
@@ -90,6 +81,8 @@
     }
     for name in ORDER:
         loads[name].start()
+    live_load = pltpu.make_async_copy(r.live_in, r.live, r.load_sem.at[len(ORDER)])
+    live_load.start()
     each(ng, g, lambda t: greet(*layer_place(t)))
     each(nz, z, lambda t: greet(2 * t + core, j))
 
@@ -253,6 +246,7 @@
     loads["snd"].wait()
     loads["rcv"].wait()
     per = tile // W
+    live_load.wait()
     alive = r.live[0]
 
     def sender_row(t):
@@ -576,7 +570,8 @@
         back_got=pltpu.VMEM((4, W, W), BF16),
         bias_rows=pltpu.VMEM((b_rows, W), F32),
         b_flat=pltpu.VMEM((3 * W + b_rows, W), F32),
-        load_sem=pltpu.SemaphoreType.DMA((len(INPUTS),)),
+        live=pltpu.SMEM((1,), I32),
+        load_sem=pltpu.SemaphoreType.DMA((len(INPUTS) + 1,)),
         halo_sem=pltpu.SemaphoreType.DMA((2, 4)),
         back_sem=pltpu.SemaphoreType.DMA((2, 4)),
         cot_sem=pltpu.SemaphoreType.DMA((2,)),
@@ -596,14 +591,13 @@
             name + "_z_sem": pltpu.SemaphoreType.DMA((2,)),
             name + "_ag_sem": pltpu.SemaphoreType.DMA((2,)),
         }
-    names = tuple(name + "_in" for name in INPUTS) + ("live",)
+    names = tuple(name + "_in" for name in INPUTS) + ("live_in",)
     names += tuple(name + "_out" for name in OUTPUTS) + tuple(scratch)
-    smem = pl.BlockSpec(memory_space=pltpu.SMEM)
     hbm = pl.BlockSpec(memory_space=pltpu.HBM)
     outs = pl.pallas_call(
         functools.partial(kernel, dims, names),
         out_shape=shapes,
-        in_specs=[hbm] * len(INPUTS) + [smem],
+        in_specs=[hbm] * (len(INPUTS) + 1),
         out_specs=(hbm,) * 5,
         scratch_shapes=list(scratch.values()),
         compiler_params=pltpu.CompilerParams(

time: 76.5 us -> 76.6 us (level)
  no operation moved by 1% of the time
where the time goes in v6:
time: 76.6 us; the launch traced here: 76.4 us
  Pallas kernels  75.1 us (98%)
  between operations  1.29 us (2%)
    pallas_call x1, Pallas kernels, body(): pl.pallas_call(functools.partial(kernel, dims, names), out_shape=shapes,...  72.7 us
    pallas_call x1, Pallas kernels, body(): pl.pallas_call(functools.partial(settle, cuts), out_shape=shapes, in_spec...  2.44 us

profile of v6, /device:TPU:1, one launch (start us, length us, event | category | flops | bytes accessed | tf_op | source)
XLA Modules:
  0.0 76.4 jit_solution(4510948838349017576)
XLA Ops:
  1.3 72.7 %mesh_step.1 = (bf16[1024,128]{1,0:T(8,128)(2,1)}, bf16[1024,128]{1,0:T(8,128)(2,1)}, bf16[4096,128]{1,0:T(8,128)(2,1)}, f32[1152,128]{1,0:T(8,128)}, f32[3,128]{1,0:T(4,128)}) custom-call(bf16[1024,128]{1,0:T(8,128)(2,1)} %refs_0_.1, bf16[4096,128]{1,0:T(8,128)(2,1)} %refs_1_.1, s32[32,128]{1,0:T(8,128)} %bitcast.6, s32[32,128]{1,0:T(8,128)} %bitcast.7, ...), custom_call_target="tpu_custom_call" | custom-call | flops 8053063680 | bytes 3145728 | tf_op jit(solution)/shard_map/mesh_step/pallas_call | solution.py:597
  74.0 2.4 %settle.1 = (bf16[1024,128]{1,0:T(8,128)(2,1)}, bf16[1024,128]{1,0:T(8,128)(2,1)}, bf16[4096,128]{1,0:T(8,128)(2,1)}, f32[1152,128]{1,0:T(8,128)}, f32[3,128]{1,0:T(4,128)}) custom-call(bf16[1024,128]{1,0:T(8,128)(2,1)} %get-tuple-element.15.refs_0_, bf16[1024,128]{1,0:T(8,128)(2,1)} %get-tuple-element.16.refs_1_, ...), custom_call_target="tpu_custom_call" | custom-call | tf_op jit(solution)/shard_map/settle/pallas_call | solution.py:614

commit v7 on v5

--- a/solution.py
+++ b/solution.py
@@ -273,7 +273,7 @@
         r.marks[t, half_e:, :] = hot(folded(receiver_row(t), half_c), half_c)
         return c
 
-    lax.fori_loop(0, tiles, mark, 0)
+    mark(0, 0)
 
     loads["w_edge"].wait()
     loads["bias"].wait()
@@ -294,7 +294,7 @@
     r.h_acc[...] = jnp.zeros_like(r.h_acc)
 
     def edge_rows(t):
-        return pl.ds(pl.multiple_of(t * tile, tile), tile)
+        return pl.ds(t * tile if isinstance(t, int) else pl.multiple_of(t * tile, tile), tile)
 
     def forward(t, c):
         above = high_r(t)
@@ -308,7 +308,10 @@
         r.h_acc[...] += right_t(r.marks[t, half_e:, :], halves(above, pre * sigma))
         return c
 
-    lax.fori_loop(0, tiles, forward, 0, unroll=2)
+    for t in range(tiles):
+        if t + 1 < tiles:
+            mark(t + 1, 0)
+        forward(t, 0)
 
     loads["w_node"].wait()
     loads["w_coarse"].wait()
@@ -405,7 +408,8 @@
         leaving[-1].start()
 
     half = tiles // 2
-    lax.fori_loop(0, tiles, backward, 0, unroll=2)
+    for t in range(tiles):
+        backward(t, 0)
     a_stage.to_column()
 
     s_bf = unfold(r.s_acc[...]).astype(BF16)

time: 76.5 us -> 75.4 us (0.986)
  Pallas kernels: 75.1 us -> 73.8 us
    pallas_call x1, Pallas kernels: 72.6 us -> 71.3 us  [body(): pl.pallas_call(functools.partial(kernel, dims, names), out_shape=shapes,...]
where the time goes in v7:
time: 75.4 us; the launch traced here: 75.2 us
  Pallas kernels  73.8 us (98%)
  between operations  1.45 us (2%)
    pallas_call x1, Pallas kernels, body(): pl.pallas_call(functools.partial(kernel, dims, names), out_shape=shapes,...  71.3 us
    pallas_call x1, Pallas kernels, body(): pl.pallas_call(functools.partial(settle, cuts), out_shape=shapes, in_spec...  2.44 us

profile of v7, /device:TPU:1, one launch (start us, length us, event | category | flops | bytes accessed | tf_op | source)
XLA Modules:
  0.0 75.2 jit_solution(7155989713094440662)
XLA Ops:
  1.3 71.3 %mesh_step.1 = (bf16[1024,128]{1,0:T(8,128)(2,1)}, bf16[1024,128]{1,0:T(8,128)(2,1)}, bf16[4096,128]{1,0:T(8,128)(2,1)}, f32[1152,128]{1,0:T(8,128)}, f32[3,128]{1,0:T(4,128)}) custom-call(bf16[1024,128]{1,0:T(8,128)(2,1)} %refs_0_.1, bf16[4096,128]{1,0:T(8,128)(2,1)} %refs_1_.1, s32[32,128]{1,0:T(8,128)} %bitcast.6, s32[32,128]{1,0:T(8,128)} %bitcast.7, ...), custom_call_target="tpu_custom_call" | custom-call | flops 8053063680 | bytes 3145728 | tf_op jit(solution)/shard_map/mesh_step/pallas_call | solution.py:607
  72.6 2.4 %settle.1 = (bf16[1024,128]{1,0:T(8,128)(2,1)}, bf16[1024,128]{1,0:T(8,128)(2,1)}, bf16[4096,128]{1,0:T(8,128)(2,1)}, f32[1152,128]{1,0:T(8,128)}, f32[3,128]{1,0:T(4,128)}) custom-call(bf16[1024,128]{1,0:T(8,128)(2,1)} %get-tuple-element.15.refs_0_, bf16[1024,128]{1,0:T(8,128)(2,1)} %get-tuple-element.16.refs_1_, ...), custom_call_target="tpu_custom_call" | custom-call | tf_op jit(solution)/shard_map/settle/pallas_call | solution.py:624

commit v8 on v7

--- a/solution.py
+++ b/solution.py
@@ -67,11 +67,11 @@
         some = 5 if count > 5 else 1
         first = 1 + (count - 1) % some
         for d in range(1, first):
-            action(me ^ d)
+            action(me ^ (count - d))
 
         def step(k, c):
             for u in range(some):
-                action(me ^ (first + k * some + u))
+                action(me ^ (count - first - k * some - u))
             return c
 
         lax.fori_loop(0, (count - first) // some, step, 0)
@@ -190,9 +190,11 @@
     def pick_half(high, both):
         return jnp.where(high, both[W:, :], both[:W, :])
 
-    def halves(high, value):
-        low = jnp.where(high, 0.0, value)
-        return jnp.concatenate([low, value - low], axis=0).astype(BF16)
+    def halves(line, half, value):
+        high = jnp.where(line >= half, 1.0, 0.0)
+        low = jnp.broadcast_to((1.0 - high).astype(BF16), value.shape)
+        high = jnp.broadcast_to(high.astype(BF16), value.shape)
+        return jnp.concatenate([value * low, value * high], axis=0)
 
     def unfold(pairs):
         return jnp.concatenate([pairs[:, :W], pairs[:, W:]], axis=0)
@@ -281,6 +283,8 @@
     b_col = jnp.broadcast_to(r.bias[0:1, :], (W, W)).T
     r.table_t[:, half_e:] = fold_t(dot(wr_t, r.ext_t[:, :cells]), half_c).astype(BF16)
     loads["feat"].wait()
+    loads["w_node"].wait()
+    loads["w_coarse"].wait()
     for copy in halo_out:
         copy.wait_recv()
     for k in range(4):
@@ -305,7 +309,7 @@
         )
         sigma = sigmoid(pre)
         r.slopes[t] = slope(pre, sigma)
-        r.h_acc[...] += right_t(r.marks[t, half_e:, :], halves(above, pre * sigma))
+        r.h_acc[...] += right_t(r.marks[t, half_e:, :], halves(receiver_row(t), half_c, (pre * sigma).astype(BF16)))
         return c
 
     for t in range(tiles):
@@ -313,8 +317,6 @@
             mark(t + 1, 0)
         forward(t, 0)
 
-    loads["w_node"].wait()
-    loads["w_coarse"].wait()
     r.hb[...] = unfold(r.h_acc[...]).astype(BF16)
     r.agg[...] = dot(r.hb[...], r.w_edge[3]).astype(BF16)
     pre_node = dot(r.nodes[...], r.w_node[0]) + dot(r.agg[...], r.w_node[1]) + r.bias[1:2, :]
@@ -392,8 +394,8 @@
         d_pre = got * r.slopes[t]
         d_pre_bf = d_pre.astype(BF16)
         r.d_pre[t] = d_pre_bf
-        r.s_acc[...] += right_t(r.marks[t, :half_e, :], halves(high_s(t), d_pre))
-        r.r_acc[...] += right_t(r.marks[t, half_e:, :], halves(above, d_pre))
+        r.s_acc[...] += right_t(r.marks[t, :half_e, :], halves(sender_row(t), half_e, d_pre_bf))
+        r.r_acc[...] += right_t(r.marks[t, half_e:, :], halves(receiver_row(t), half_c, d_pre_bf))
         r.we_acc[...] += dot(d_pre_bf, r.feat[edge_rows(t), :])
         return c
 

time: 75.4 us -> 71.3 us (0.946)
  Pallas kernels: 73.8 us -> 69.7 us
    pallas_call x1, Pallas kernels: 71.3 us -> 67.2 us  [body(): pl.pallas_call(functools.partial(kernel, dims, names), out_shape=shapes,...]
where the time goes in v8:
time: 71.3 us; the launch traced here: 71.1 us
  Pallas kernels  69.7 us (98%)
  between operations  1.45 us (2%)
    pallas_call x1, Pallas kernels, body(): pl.pallas_call(functools.partial(kernel, dims, names), out_shape=shapes,...  67.2 us
    pallas_call x1, Pallas kernels, body(): pl.pallas_call(functools.partial(settle, cuts), out_shape=shapes, in_spec...  2.44 us

profile of v8, /device:TPU:1, one launch (start us, length us, event | category | flops | bytes accessed | tf_op | source)
XLA Modules:
  0.0 71.1 jit_solution(8300267761617212625)
XLA Ops:
  1.3 67.2 %mesh_step.1 = (bf16[1024,128]{1,0:T(8,128)(2,1)}, bf16[1024,128]{1,0:T(8,128)(2,1)}, bf16[4096,128]{1,0:T(8,128)(2,1)}, f32[1152,128]{1,0:T(8,128)}, f32[3,128]{1,0:T(4,128)}) custom-call(bf16[1024,128]{1,0:T(8,128)(2,1)} %refs_0_.1, bf16[4096,128]{1,0:T(8,128)(2,1)} %refs_1_.1, s32[32,128]{1,0:T(8,128)} %bitcast.6, s32[32,128]{1,0:T(8,128)} %bitcast.7, ...), custom_call_target="tpu_custom_call" | custom-call | flops 8053063680 | bytes 3145728 | tf_op jit(solution)/shard_map/mesh_step/pallas_call | solution.py:609
  68.5 2.4 %settle.1 = (bf16[1024,128]{1,0:T(8,128)(2,1)}, bf16[1024,128]{1,0:T(8,128)(2,1)}, bf16[4096,128]{1,0:T(8,128)(2,1)}, f32[1152,128]{1,0:T(8,128)}, f32[3,128]{1,0:T(4,128)}) custom-call(bf16[1024,128]{1,0:T(8,128)(2,1)} %get-tuple-element.15.refs_0_, bf16[1024,128]{1,0:T(8,128)(2,1)} %get-tuple-element.16.refs_1_, ...), custom_call_target="tpu_custom_call" | custom-call | tf_op jit(solution)/shard_map/settle/pallas_call | solution.py:626

commit v9 on v8

--- a/solution.py
+++ b/solution.py
@@ -203,8 +203,10 @@
         return jnp.concatenate([table[:, :half], table[:, half:]], axis=0)
 
     def to_coarse(value):
-        low = jnp.where(r.own_high[...] > 0.5, 0.0, value)
-        pairs = jnp.concatenate([low, value - low], axis=1).astype(BF16)
+        high = r.own_high[...]
+        pairs = jnp.concatenate(
+            [value * (1.0 - high).astype(BF16), value * high.astype(BF16)], axis=1
+        )
         return unfold(dot(r.own_t[...], pairs)).astype(BF16).reshape(ny, owned, W)
 
     def from_coarse(table):
@@ -244,7 +246,7 @@
         r.own_at[q * W : (q + 1) * W, :] = at
     r.own_high[...] = jnp.where(r.own_at[...] >= float(half_c), 1.0, 0.0)
     loads["cot"].wait()
-    r.cot_src[...] = to_coarse(r.cot[...].astype(F32))
+    r.cot_src[...] = to_coarse(r.cot[...])
 
     pl.semaphore_wait(barrier, ng + nz - 1)
     halo_out = halo_copies(r.pick, r.halo, r.halo_sem)
@@ -324,7 +326,7 @@
     r.node_slope[...] = slope(pre_node, sigma)
     r.hid[...] = (pre_node * sigma).astype(BF16)
     r.fine[...] = r.nodes[...].astype(F32) + dot(r.hid[...], r.w_node[2])
-    r.fine_src[...] = to_coarse(r.fine[...])
+    r.fine_src[...] = to_coarse(r.fine[...].astype(BF16))
     row.scatter(r.fine_src, r.fine_got, r.fine_sem)
 
     lanes = lax.broadcasted_iota(I32, (cells, W), 1).astype(F32)

time: 71.3 us -> 71.3 us (level)
  no operation moved by 1% of the time
where the time goes in v9:
time: 71.3 us; the launch traced here: 71.2 us
  Pallas kernels  69.7 us (98%)
  between operations  1.45 us (2%)
    pallas_call x1, Pallas kernels, body(): pl.pallas_call(functools.partial(kernel, dims, names), out_shape=shapes,...  67.3 us
    pallas_call x1, Pallas kernels, body(): pl.pallas_call(functools.partial(settle, cuts), out_shape=shapes, in_spec...  2.44 us

profile of v9, /device:TPU:1, one launch (start us, length us, event | category | flops | bytes accessed | tf_op | source)
XLA Modules:
  0.0 71.2 jit_solution(2231472801049379445)
XLA Ops:
  1.3 67.3 %mesh_step.1 = (bf16[1024,128]{1,0:T(8,128)(2,1)}, bf16[1024,128]{1,0:T(8,128)(2,1)}, bf16[4096,128]{1,0:T(8,128)(2,1)}, f32[1152,128]{1,0:T(8,128)}, f32[3,128]{1,0:T(4,128)}) custom-call(bf16[1024,128]{1,0:T(8,128)(2,1)} %refs_0_.1, bf16[4096,128]{1,0:T(8,128)(2,1)} %refs_1_.1, s32[32,128]{1,0:T(8,128)} %bitcast.6, s32[32,128]{1,0:T(8,128)} %bitcast.7, ...), custom_call_target="tpu_custom_call" | custom-call | flops 8053063680 | bytes 3145728 | tf_op jit(solution)/shard_map/mesh_step/pallas_call | solution.py:611
  68.6 2.4 %settle.1 = (bf16[1024,128]{1,0:T(8,128)(2,1)}, bf16[1024,128]{1,0:T(8,128)(2,1)}, bf16[4096,128]{1,0:T(8,128)(2,1)}, f32[1152,128]{1,0:T(8,128)}, f32[3,128]{1,0:T(4,128)}) custom-call(bf16[1024,128]{1,0:T(8,128)(2,1)} %get-tuple-element.15.refs_0_, bf16[1024,128]{1,0:T(8,128)(2,1)} %get-tuple-element.16.refs_1_, ...), custom_call_target="tpu_custom_call" | custom-call | tf_op jit(solution)/shard_map/settle/pallas_call | solution.py:628
